TPU v7x, 128 devices: a whole 4x4x4 slice. The times are simulated.
128 devices in a mesh: sx: 8 (over x, core), sy: 16 (over y, z).
Axes of the slice: x: 4, y: 4, z: 4, core: 2. Of those that a mesh axis runs over, the one named last changes fastest.
Arguments:
- weights: float32 [2, 256, 256, 256], P(None, 'sx', 'sy'), may hold values from -0.125 to 0.125
Outputs:
- target_weights: float32 [2, 256, 256, 256], P(None, 'sx', 'sy')
All inputs are finite; a program needn't handle non-finite values.
Results may differ from a plain program's by a relative error of at most 0.0015.
Values sent between devices are 32-bit elements; how exact they have to be, the bound alone decides.
No kernel may reach another device: no remote copies, remote signals or barrier semaphores. Data moves between devices by JAX's collectives and lax.ppermute only.
A program may use at most 128 MiB of HBM per device.

v0:
```python
import functools
import math

import jax
import jax.numpy as jnp
import ml_dtypes
import numpy as np
from jax import lax
from jax.experimental import pallas as pl
from jax.experimental.pallas import tpu as pltpu
from jax.sharding import PartitionSpec as P

CHEB = 8
RANK = 64
GRID = 4096
LEVELS = 8
START = 2
HALF = 4
LANES = 2 * RANK
F32 = jnp.float32
BF16 = jnp.bfloat16
MIB = 1 << 20

SIN_TERMS = (6.283184916, -41.34158923, 81.59994333, -76.61447253, 41.34288235, -12.47124353)
COS_TERMS = (0.9999999891, -19.7392045, 64.93911746, -85.45013953, 60.16763095, -25.96759925, 6.528658158)


def lagrange_tables(node_count):
    cheb_nodes = 0.5 * np.cos((2.0 * np.arange(node_count) + 1.0) * math.pi / (2.0 * node_count))
    single = np.ones((2, node_count, node_count))
    for child_bit in range(2):
        for source in range(node_count):
            location = (child_bit - 0.5) / 2.0 + cheb_nodes[source] / 2.0
            for target in range(node_count):
                for another in range(node_count):
                    if another != target:
                        single[child_bit, source, target] *= (location - cheb_nodes[another]) / (
                            cheb_nodes[target] - cheb_nodes[another]
                        )
    paired = single[:, None, :, None, :, None] * single[None, :, None, :, None, :]
    paired = paired.reshape(2, 2, node_count * node_count, node_count * node_count)
    return (cheb_nodes, paired)


def mixing_weights():
    table = lagrange_tables(CHEB)[1].astype(np.float32).reshape(4, RANK, RANK)
    high = table.astype(ml_dtypes.bfloat16)
    low = (table - high.astype(np.float32)).astype(ml_dtypes.bfloat16)
    out = np.zeros((4, 2, LANES, 2, LANES), ml_dtypes.bfloat16)
    for half in range(2):
        part = slice(half * RANK, (half + 1) * RANK)
        for split in range(2):
            out[:, split, part, 0, part] = high
            out[:, split, part, 1, part] = low
    return out.reshape(4 * 2 * LANES, 2 * LANES)


def node_lanes():
    nodes = lagrange_tables(CHEB)[0].astype(np.float32)
    lane = np.arange(LANES) % RANK
    out = np.zeros((8, LANES), np.float32)
    out[0] = nodes[lane // CHEB]
    out[1] = nodes[lane % CHEB]
    return out


def poly(terms, u):
    acc = terms[-1] * u + terms[-2]
    for term in terms[-3::-1]:
        acc = acc * u + term
    return acc


def sin_turns(f):
    return f * poly(SIN_TERMS, f * f)


def cos_sin(turns):
    f = turns - jnp.round(turns)
    u = f * f
    return poly(COS_TERMS, u), f * poly(SIN_TERMS, u)


def reversed_bits(values, count):
    out = jnp.zeros_like(values)
    for bit in range(count):
        out = out + (((values >> bit) & 1) << (count - 1 - bit))
    return out


def dim_tables(j, after, index, dim, nodes_ref):
    row = lax.broadcasted_iota(jnp.int32, (16, LANES), 0)
    lane = lax.broadcasted_iota(jnp.int32, (16, LANES), 1)
    half = (lane >= RANK).astype(jnp.int32)
    if dim == 0:
        g = row * 16 + half * 8 + index if after else index * 32 + half * 16 + row
    else:
        g = row * 16 + index if after else index * 16 + row
    z = jnp.broadcast_to(nodes_ref[dim : dim + 1, :], (16, LANES))
    b = g >> j
    p = reversed_bits(g & ((1 << j) - 1), j)
    level = START + j
    width = 2.0**level
    wave = (-GRID / 2.0 + (b.astype(F32) + 0.5) * width) + width * z
    odd = ((2 * b + 1) & 7).astype(F32) * 0.125
    linear = odd + 0.25 * z
    p = p.astype(F32)
    parent = sin_turns((p + 0.5) * 0.5**level)
    new = [sin_turns((2.0 * p + (s + 0.5)) * 0.5 ** (level + 1)) for s in range(2)]
    if j == 0:
        lin = []
        for s in range(2):
            whole = (((2 * b + 1) * (2 * s + 1)) & 7).astype(F32) * 0.125
            lin.append(-(whole + ((2 * s + 1) * 0.25) * z))
    else:
        lin = [linear, -linear]
    return wave, lin, parent, new


def store_tables(ref, dim, tables):
    wave, lin, parent, new = tables
    for k, value in enumerate((wave, lin[0], lin[1], parent, new[0], new[1])):
        ref[dim, k] = value


def fill_phases(j, after, index_one, index_two, nodes_ref, tab_ref, store):
    store_tables(tab_ref, 0, dim_tables(j, after, index_one, 0, nodes_ref))
    store_tables(tab_ref, 1, dim_tables(j, after, index_two, 1, nodes_ref))

    @pl.loop(0, 16)
    def _(i1):
        def one(k):
            return jnp.broadcast_to(tab_ref[0, k, pl.ds(i1, 1), :], (8, LANES))

        wave1 = one(0)
        wave1 = wave1 * wave1
        lin1 = (one(1), one(2))
        par1, new1 = one(3) * 0.0625, (one(4) * 0.0625, one(5) * 0.0625)
        for h in range(2):

            def two(k):
                return tab_ref[1, k, 8 * h : 8 * h + 8, :]

            wave2 = two(0)
            radius = jnp.sqrt(wave1 + wave2 * wave2)
            lin2 = (two(1), two(2))
            par = par1 * two(3)
            for s1 in range(2):
                for s2 in range(2):
                    new = new1[s1] * two(4 + s2)
                    bend = -(0.125 + new) if j == 0 else par - new
                    turns = bend * radius + (lin1[s1] + lin2[s2])
                    cos, sin = cos_sin(turns)
                    store(i1, 2 * s1 + s2, h, cos, sin)


def phase_rows(i1, s, h):
    return pl.ds(pl.multiple_of((i1 * 4 + s) * 16 + 8 * h, 8), 8)


def fill_final(index_one, index_two, nodes_ref, tab_ref, store):
    row = lax.broadcasted_iota(jnp.int32, (16, LANES), 0)
    lane = lax.broadcasted_iota(jnp.int32, (16, LANES), 1)
    half = (lane >= RANK).astype(jnp.int32)
    for dim in range(2):
        g = row * 16 + half * 8 + index_one if dim == 0 else row * 16 + index_two
        z = jnp.broadcast_to(nodes_ref[dim : dim + 1, :], (16, LANES))
        p = 2 * reversed_bits(g, LEVELS) + 1
        level = START + LEVELS
        wave = (-GRID / 2.0 + 0.5 * 2.0**level) + 2.0**level * z
        whole = ((-3 * p) & 3).astype(F32) * 0.25
        tab_ref[dim, 0] = wave
        tab_ref[dim, 1] = whole + (p.astype(F32) * 0.5) * z
        tab_ref[dim, 2] = sin_turns(p.astype(F32) * 0.5 ** (level + 1))

    @pl.loop(0, 16)
    def _(i1):
        def one(k):
            return jnp.broadcast_to(tab_ref[0, k, pl.ds(i1, 1), :], (8, LANES))

        wave1, lin1, sin1 = one(0), one(1), one(2) * 0.0625
        for h in range(2):
            rows = slice(8 * h, 8 * h + 8)
            wave2 = tab_ref[1, 0, rows, :]
            radius = jnp.sqrt(wave1 * wave1 + wave2 * wave2)
            bend = 0.125 + sin1 * tab_ref[1, 2, rows, :]
            turns = bend * radius + (lin1 + tab_ref[1, 1, rows, :])
            turns = turns - jnp.round(turns)
            cos, sin = cos_sin(turns)
            store(i1, h, cos, sin)


def insert(rest, bit, value):
    low = rest & ((1 << bit) - 1)
    return ((rest >> bit) << (bit + 1)) + (value << bit) + low


def turn_signs():
    row = lax.broadcasted_iota(jnp.int32, (8, LANES), 0)
    return jnp.where(row < 4, -1.0, 1.0).astype(F32)


def level(bit, place, load, cos_of, sin_of, lhs_ref, w_ref, emit):
    signs = turn_signs()

    @pl.loop(0, 8)
    def _(r1):
        for r2 in range(8):
            for c in range(4):
                i1 = insert(r1, bit, c >> 1)
                i2 = insert(r2, bit, c & 1)
                value = load(place(i1, i2))
                turned = pltpu.roll(value, 4, 0) * signs
                for s1 in range(2):
                    parts = []
                    for s2 in range(2):
                        row = (i1 * 4 + (2 * s1 + s2)) * 16 + i2
                        cos = cos_of(row)
                        sin = sin_of(row)
                        parts.append(value * cos + turned * sin)
                    both = jnp.concatenate(parts, axis=0)
                    high = both.astype(BF16)
                    low = (both - high.astype(F32)).astype(BF16)
                    start = pl.multiple_of(r1 * 256 + (r2 * 2 + s1) * 16, 16)
                    lhs_ref[pl.ds(start, 16), 256 * c : 256 * c + 128] = high
                    lhs_ref[pl.ds(start, 16), 256 * c + 128 : 256 * c + 256] = low

    @pl.loop(0, 4)
    def _(block):
        y = jnp.dot(
            lhs_ref[pl.ds(pl.multiple_of(block * 512, 512), 512), :],
            w_ref[...],
            preferred_element_type=F32,
        )
        y = y[:, :LANES] + y[:, LANES:]
        for q in range(2):
            r1 = block * 2 + q
            for r2 in range(8):
                base = (q * 8 + r2) * 32
                new = [y[base + 8 * s : base + 8 * s + 8] for s in range(4)]
                emit(r1, r2, new)


def before_kernel(x_ref, w_ref, nodes_ref, out_ref, d0, d1, cos_ref, sin_ref, tab_ref, lhs_ref):
    index_one = lax.axis_index("sx")
    index_two = lax.axis_index("sy")
    lower = lax.broadcasted_iota(jnp.int32, (8, LANES), 1) < RANK

    @pl.loop(0, 16)
    def _(i1):
        for part in range(2):
            for h in range(2):
                for pair in range(2):
                    cols = slice(pair * LANES, (pair + 1) * LANES)
                    a = x_ref[part, pl.ds(i1, 1), 8 * h : 8 * h + 8, cols].reshape(8, LANES)
                    b = x_ref[part, pl.ds(i1 + 16, 1), 8 * h : 8 * h + 8, cols].reshape(8, LANES)
                    start = (i1 * 16 + 8 * h) * 8 + part * 4 + 2 * pair
                    d0[pl.ds(start, 8, stride=8), :] = jnp.where(lower, a, pltpu.roll(b, RANK, 1))
                    d0[pl.ds(start + 1, 8, stride=8), :] = jnp.where(lower, pltpu.roll(a, RANK, 1), b)

    def place(i1, i2):
        return i1 * 16 + i2

    refs = (d0, d1)
    for j in range(HALF):

        def store(i1, s, h, cos, sin):
            cos_ref[phase_rows(i1, s, h), :] = cos
            sin_ref[phase_rows(i1, s, h), :] = sin

        fill_phases(j, False, index_one, index_two, nodes_ref, tab_ref, store)
        source, target = refs[j % 2], refs[(j + 1) % 2]

        def load(pos):
            return source[pl.ds(pl.multiple_of(pos * 8, 8), 8), :]

        def emit(r1, r2, new):
            if j < HALF - 1:
                for s in range(4):
                    pos = place(insert(r1, j, s >> 1), insert(r2, j, s & 1))
                    target[pl.ds(pl.multiple_of(pos * 8, 8), 8), :] = new[s]
            else:
                for s2 in range(2):
                    a, b = new[s2], new[2 + s2]
                    pos = ((r1 * 16 + insert(r2, j, s2)) * 2) * 8
                    first = jnp.where(lower, a, pltpu.roll(b, RANK, 1))
                    second = jnp.where(lower, pltpu.roll(a, RANK, 1), b)
                    out_ref[pl.ds(pl.multiple_of(pos, 8), 8), :] = first
                    out_ref[pl.ds(pl.multiple_of(pos + 8, 8), 8), :] = second

        level(
            j,
            place,
            load,
            lambda row: cos_ref[pl.ds(row, 1), :],
            lambda row: sin_ref[pl.ds(row, 1), :],
            lhs_ref,
            w_ref,
            emit,
        )


def phases_kernel(nodes_ref, cos_ref, sin_ref, cosf_ref, sinf_ref, tab_ref):
    index_one = lax.axis_index("sx")
    index_two = lax.axis_index("sy")
    for step in range(LEVELS - HALF):

        def store(i1, s, h, cos, sin):
            cos_ref[step, phase_rows(i1, s, h), :] = cos
            sin_ref[step, phase_rows(i1, s, h), :] = sin

        fill_phases(HALF + step, True, index_one, index_two, nodes_ref, tab_ref, store)

    def store_final(i1, h, cos, sin):
        rows = pl.ds(pl.multiple_of(i1 * 16 + 8 * h, 8), 8)
        cosf_ref[rows, :] = cos
        sinf_ref[rows, :] = sin

    fill_final(index_one, index_two, nodes_ref, tab_ref, store_final)


def after_kernel(x_ref, w_ref, cos_ref, sin_ref, cosf_ref, sinf_ref, out_ref, d0, d1, lhs_ref):
    def place(i1, i2):
        return (i1 >> 1) * 32 + i2 * 2 + (i1 & 1)

    signs = turn_signs()
    refs = (x_ref, d0, d1, d0, out_ref)
    for step in range(LEVELS - HALF):
        source, target = refs[step], refs[step + 1]

        def load(pos):
            return source[pl.ds(pl.multiple_of(pos * 8, 8), 8), :]

        def emit(r1, r2, new):
            for s in range(4):
                i1, i2 = insert(r1, step, s >> 1), insert(r2, step, s & 1)
                value = new[s]
                if step == LEVELS - HALF - 1:
                    row = i1 * 16 + i2
                    cos, sin = cosf_ref[pl.ds(row, 1), :], sinf_ref[pl.ds(row, 1), :]
                    value = value * cos + (pltpu.roll(value, 4, 0) * signs) * sin
                target[pl.ds(pl.multiple_of(place(i1, i2) * 8, 8), 8), :] = value

        level(
            step,
            place,
            load,
            lambda row: cos_ref[step, pl.ds(row, 1), :],
            lambda row: sin_ref[step, pl.ds(row, 1), :],
            lhs_ref,
            w_ref,
            emit,
        )


def order_kernel(x_ref, out_ref):
    lower = lax.broadcasted_iota(jnp.int32, (8, LANES), 1) < RANK

    @pl.loop(0, 8)
    def _(sx):
        for b4 in range(2):
            for part in range(2):
                for pair in range(2):
                    cols = slice(pair * LANES, (pair + 1) * LANES)
                    for h in range(2):
                        start = ((sx * 16 + 8 * h) * 2 + b4) * 8 + part * 4 + 2 * pair
                        a = x_ref[pl.ds(start, 8, stride=16), :]
                        b = x_ref[pl.ds(start + 1, 8, stride=16), :]
                        first = jnp.where(lower, a, pltpu.roll(b, RANK, 1))
                        second = jnp.where(lower, pltpu.roll(a, RANK, 1), b)
                        rows = slice(8 * h, 8 * h + 8)
                        out_ref[part, pl.ds(b4 * 16 + sx, 1), rows, cols] = first[None]
                        out_ref[part, pl.ds(b4 * 16 + 8 + sx, 1), rows, cols] = second[None]


VMEM = pl.BlockSpec(memory_space=pltpu.VMEM)
ROWS = 2048


def local(weights):
    w = jnp.asarray(mixing_weights())
    nodes = jnp.asarray(node_lanes())
    shape = jax.ShapeDtypeStruct((ROWS, LANES), F32)
    values = pltpu.VMEM((ROWS, LANES), F32)
    table = pltpu.VMEM((2, 6, 16, LANES), F32)
    lhs = pltpu.VMEM((2048, 1024), BF16)
    cost = functools.partial(pl.CostEstimate, transcendentals=0)

    before = pl.pallas_call(
        before_kernel,
        out_shape=shape,
        in_specs=[VMEM] * 3,
        out_specs=VMEM,
        scratch_shapes=[values, values, pltpu.VMEM((1024, LANES), F32), pltpu.VMEM((1024, LANES), F32), table, lhs],
        compiler_params=pltpu.CompilerParams(vmem_limit_bytes=24 * MIB),
        cost_estimate=cost(flops=4 * 2**31, bytes_accessed=3 * MIB),
        name="before",
    )(weights, w, nodes)

    moved = lax.all_to_all(before.reshape(128, 16, LANES), ("sx", "sy"), 0, 0, tiled=True)

    phase = jax.ShapeDtypeStruct((LEVELS - HALF, 1024, LANES), F32)
    last = jax.ShapeDtypeStruct((256, LANES), F32)
    phases = pl.pallas_call(
        phases_kernel,
        out_shape=(phase, phase, last, last),
        in_specs=[VMEM],
        out_specs=(VMEM,) * 4,
        scratch_shapes=[table],
        compiler_params=pltpu.CompilerParams(vmem_limit_bytes=24 * MIB),
        cost_estimate=cost(flops=2**33, bytes_accessed=5 * MIB),
        name="phases",
    )(nodes)

    after = pl.pallas_call(
        after_kernel,
        out_shape=shape,
        in_specs=[VMEM] * 6,
        out_specs=VMEM,
        scratch_shapes=[values, values, lhs],
        compiler_params=pltpu.CompilerParams(vmem_limit_bytes=24 * MIB),
        cost_estimate=cost(flops=4 * 2**31, bytes_accessed=8 * MIB),
        name="after",
    )(moved.reshape(ROWS, LANES), w, *phases)

    moved = lax.all_to_all(after.reshape(128, 16, LANES), ("sx", "sy"), 0, 0, tiled=True)

    return pl.pallas_call(
        order_kernel,
        out_shape=jax.ShapeDtypeStruct(weights.shape, F32),
        in_specs=[VMEM],
        out_specs=VMEM,
        compiler_params=pltpu.CompilerParams(vmem_limit_bytes=8 * MIB),
        cost_estimate=cost(flops=2**20, bytes_accessed=2 * MIB),
        name="order",
    )(moved.reshape(ROWS, LANES))


def solution(mesh):
    return jax.shard_map(
        local,
        mesh=mesh,
        in_specs=(P(None, "sx", "sy", None),),
        out_specs=P(None, "sx", "sy", None),
        check_vma=False,
    )
```

profile of v0, /device:TPU:1, one launch (start us, length us, event | category | flops | bytes accessed | tf_op | source)
XLA Modules:
  0.0 90.0 jit_solution(2990830567611416439)
XLA Ops:
  0.0 0.0 copy-start
  0.0 1.2 %copy-done = f32[2,32,16,256]{3,2,1,0:T(8,128)S(1)} copy-done((f32[2,32,16,256]{3,2,1,0:T(8,128)S(1)}, f32[2,32,16,256]{3,2,1,0:T(8,128)}, u32[]{:S(2)}) %copy-start) | copy-done | bytes 1048600
  1.2 0.0 copy-start.1
  1.2 1.0 %copy-done.1 = bf16[1024,256]{1,0:T(8,128)(2,1)S(1)} copy-done((bf16[1024,256]{1,0:T(8,128)(2,1)S(1)}, bf16[1024,256]{1,0:T(8,128)(2,1)}, u32[]{:S(2)}) %copy-start.1) | copy-done | bytes 524312
  2.3 0.0 copy-start.3
  2.3 0.7 copy-done.3
  3.0 16.9 %before.1 = f32[2048,128]{1,0:T(8,128)} custom-call(f32[2,32,16,256]{3,2,1,0:T(8,128)S(1)} %copy-done, bf16[1024,256]{1,0:T(8,128)(2,1)S(1)} %copy-done.1, f32[8,128]{1,0:T(8,128)S(1)} %copy-done.3), custom_call_target="tpu_custom_call" | custom-call | flops 8589934592 | bytes 3145728 | tf_op jit(solution)/shard_map/before/pallas_call | solution.py:389
  19.9 0.0 copy-start.4
  19.9 11.5 %all-to-all-start = ((f32[128,16,128]{2,1,0:T(8,128)}), f32[128,16,128]{2,1,0:T(8,128)S(1)}, u32[]{:S(2)}, u32[]{:S(2)}) async-start(f32[128,16,128]{2,1,0:T(8,128)} %bitcast), calls=%async_computation | async-start | bytes 2097152 | tf_op jit(solution)/shard_map/all_to_all | solution.py:400
  31.4 0.0 copy-done.4
  31.4 0.0 copy-start.2
  31.4 3.9 %phases.1 = (f32[4,1024,128]{2,1,0:T(8,128)S(1)}, f32[4,1024,128]{2,1,0:T(8,128)S(1)}, f32[256,128]{1,0:T(8,128)S(1)}, f32[256,128]{1,0:T(8,128)S(1)}) custom-call(f32[8,128]{1,0:T(8,128)S(1)} %copy-done.4), custom_call_target="tpu_custom_call" | custom-call | flops 8589934592 | bytes 5242880 | tf_op jit(solution)/shard_map/phases/pallas_call | solution.py:404
  35.3 0.0 copy-start.5
  35.3 1.3 %copy-done.5 = f32[4,1024,128]{2,1,0:T(8,128)} copy-done((f32[4,1024,128]{2,1,0:T(8,128)}, f32[4,1024,128]{2,1,0:T(8,128)S(1)}, u32[]{:S(2)}) %copy-start.5) | copy-done | bytes 2097176
  36.6 0.0 copy-start.7
  36.6 1.3 %copy-done.7 = f32[4,1024,128]{2,1,0:T(8,128)} copy-done((f32[4,1024,128]{2,1,0:T(8,128)}, f32[4,1024,128]{2,1,0:T(8,128)S(1)}, u32[]{:S(2)}) %copy-start.7) | copy-done | bytes 2097176
  38.0 12.3 %all-to-all-done = f32[128,16,128]{2,1,0:T(8,128)S(1)} async-done(((f32[128,16,128]{2,1,0:T(8,128)}), f32[128,16,128]{2,1,0:T(8,128)S(1)}, u32[]{:S(2)}, u32[]{:S(2)}) %all-to-all-start) | async-done | bytes 1048608 | tf_op jit(solution)/shard_map/all_to_all | solution.py:400
  50.3 0.0 copy-done.2
  50.3 0.0 copy-start.6
  50.3 1.6 %copy-done.6 = f32[4,1024,128]{2,1,0:T(8,128)S(1)} copy-done((f32[4,1024,128]{2,1,0:T(8,128)S(1)}, f32[4,1024,128]{2,1,0:T(8,128)}, u32[]{:S(2)}) %copy-start.6) | copy-done | bytes 2097176
  51.9 0.0 copy-start.8
  51.9 1.6 %copy-done.8 = f32[4,1024,128]{2,1,0:T(8,128)S(1)} copy-done((f32[4,1024,128]{2,1,0:T(8,128)S(1)}, f32[4,1024,128]{2,1,0:T(8,128)}, u32[]{:S(2)}) %copy-start.8) | copy-done | bytes 2097176
  53.5 11.6 %after.1 = f32[2048,128]{1,0:T(8,128)S(1)} custom-call(f32[2048,128]{1,0:T(8,128)S(1)} %bitcast.5, bf16[1024,256]{1,0:T(8,128)(2,1)S(1)} %copy-done.2, f32[4,1024,128]{2,1,0:T(8,128)S(1)} %copy-done.6, f32[4,1024,128]{2,1,0:T(8,128)S(1)} %copy-done.8, f32[256,128]{1,0:T(8,128)S(1)} %get-tuple-element.11.cosf_ref, f32[256,128]{1,0:T(8,128)S(1)} %get-tuple-element.12.sinf_ref), custom_call_target="tpu_custom_call" | custom-call | flops 8589934592 | bytes 8388608 | tf_op jit(solution)/shard_map/after/pallas_call | solution.py:415
  65.1 23.1 %all_to_all.10 = f32[128,16,128]{2,1,0:T(8,128)S(1)} all-to-all(f32[128,16,128]{2,1,0:T(8,128)S(1)} %bitcast.6), channel_id=1, replica_groups=mesh['sx'=8,'sy'=16] {'sx','sy'}, dimensions={0} | all-to-all | bytes 2097152 | tf_op jit(solution)/shard_map/all_to_all | solution.py:426
  88.2 1.8 %order.1 = f32[2,32,16,256]{3,2,1,0:T(8,128)} custom-call(f32[2048,128]{1,0:T(8,128)S(1)} %bitcast.4), custom_call_target="tpu_custom_call" | custom-call | flops 1048576 | bytes 2097152 | tf_op jit(solution)/shard_map/order/pallas_call | solution.py:428
Async XLA Ops:
  0.0 1.2 %copy-start = (f32[2,32,16,256]{3,2,1,0:T(8,128)S(1)}, f32[2,32,16,256]{3,2,1,0:T(8,128)}, u32[]{:S(2)}) copy-start(f32[2,32,16,256]{3,2,1,0:T(8,128)} %x_ref.1) | copy-start | bytes 3145732
  1.2 1.0 %copy-start.1 = (bf16[1024,256]{1,0:T(8,128)(2,1)S(1)}, bf16[1024,256]{1,0:T(8,128)(2,1)}, u32[]{:S(2)}) copy-start(bf16[1024,256]{1,0:T(8,128)(2,1)} %constant.4.clone.w_ref) | copy-start | bytes 1572868
  2.3 0.7 copy-start.3
  19.9 11.5 %copy-start.4 = (f32[8,128]{1,0:T(8,128)S(1)}, f32[8,128]{1,0:T(8,128)}, u32[]{:S(2)}) copy-start(f32[8,128]{1,0:T(8,128)} %constant.5.clone.nodes_ref) | copy-start | bytes 12292
  19.9 30.4 %all-to-all-start = ((f32[128,16,128]{2,1,0:T(8,128)}), f32[128,16,128]{2,1,0:T(8,128)S(1)}, u32[]{:S(2)}, u32[]{:S(2)}) async-start(f32[128,16,128]{2,1,0:T(8,128)} %bitcast), calls=%async_computation | async-start | bytes 2097152 | tf_op jit(solution)/shard_map/all_to_all | solution.py:400
  31.4 18.9 %copy-start.2 = (bf16[1024,256]{1,0:T(8,128)(2,1)S(1)}, bf16[1024,256]{1,0:T(8,128)(2,1)}, u32[]{:S(2)}) copy-start(bf16[1024,256]{1,0:T(8,128)(2,1)} %constant.4.clone.w_ref) | copy-start | bytes 1572868
  35.3 1.3 %copy-start.5 = (f32[4,1024,128]{2,1,0:T(8,128)}, f32[4,1024,128]{2,1,0:T(8,128)S(1)}, u32[]{:S(2)}) copy-start(f32[4,1024,128]{2,1,0:T(8,128)S(1)} %get-tuple-element.9.cos_ref) | copy-start | bytes 6291460
  36.6 1.3 %copy-start.7 = (f32[4,1024,128]{2,1,0:T(8,128)}, f32[4,1024,128]{2,1,0:T(8,128)S(1)}, u32[]{:S(2)}) copy-start(f32[4,1024,128]{2,1,0:T(8,128)S(1)} %get-tuple-element.10.sin_ref) | copy-start | bytes 6291460
  50.3 1.6 %copy-start.6 = (f32[4,1024,128]{2,1,0:T(8,128)S(1)}, f32[4,1024,128]{2,1,0:T(8,128)}, u32[]{:S(2)}) copy-start(f32[4,1024,128]{2,1,0:T(8,128)} %copy-done.5) | copy-start | bytes 6291460
  51.9 1.6 %copy-start.8 = (f32[4,1024,128]{2,1,0:T(8,128)S(1)}, f32[4,1024,128]{2,1,0:T(8,128)}, u32[]{:S(2)}) copy-start(f32[4,1024,128]{2,1,0:T(8,128)} %copy-done.7) | copy-start | bytes 6291460
where the time goes:
time: 90.4 us; the launch traced here: 90 us
  Pallas kernels  34.3 us (38%)
  blocking collectives  23.1 us (26%)
  waiting for transfers between devices  12.3 us (14%)
  starting transfers between devices  11.5 us (13%)
  local copies, waits for them, and re-layouts  8.78 us (10%)
    all_to_all x1, blocking collectives, local(): lax.all_to_all(after.reshape(128, 16, LANES), ('sx', 'sy'), 0, 0, tiled=T...  23.1 us
    pallas_call x1, Pallas kernels, local(): pl.pallas_call(before_kernel, out_shape=shape, in_specs=[VMEM] * 3, out_s...  16.9 us
    all_to_all x1, waiting for transfers between devices, local(): lax.all_to_all(before.reshape(128, 16, LANES), ('sx', 'sy'), 0, 0, tiled=...  12.3 us
    pallas_call x1, Pallas kernels, local(): pl.pallas_call(after_kernel, out_shape=shape, in_specs=[VMEM] * 6, out_sp...  11.6 us
    all_to_all x1, starting transfers between devices, local(): lax.all_to_all(before.reshape(128, 16, LANES), ('sx', 'sy'), 0, 0, tiled=...  11.5 us
    unnamed x18, local copies, waits for them, and re-layouts  8.78 us
    pallas_call x1, Pallas kernels, local(): pl.pallas_call(phases_kernel, out_shape=(phase, phase, last, last), in_sp...  3.91 us
    pallas_call x1, Pallas kernels, local(): pl.pallas_call(order_kernel, out_shape=jax.ShapeDtypeStruct(weights.shape...  1.82 us
  transfers between devices with their start and end apart: 1, of which 1 were waited for; matrix products, arithmetic and copies ran while one was open for 0% of the time, Pallas kernels for 4%

commit v1 on v0

--- a/solution.py
+++ b/solution.py
@@ -20,6 +20,7 @@
 F32 = jnp.float32
 BF16 = jnp.bfloat16
 MIB = 1 << 20
+SPAN = 2
 
 SIN_TERMS = (6.283184916, -41.34158923, 81.59994333, -76.61447253, 41.34288235, -12.47124353)
 COS_TERMS = (0.9999999891, -19.7392045, 64.93911746, -85.45013953, 60.16763095, -25.96759925, 6.528658158)
@@ -55,12 +56,13 @@
     return out.reshape(4 * 2 * LANES, 2 * LANES)
 
 
-def node_lanes():
+def node_values(lane, dim):
     nodes = lagrange_tables(CHEB)[0].astype(np.float32)
-    lane = np.arange(LANES) % RANK
-    out = np.zeros((8, LANES), np.float32)
-    out[0] = nodes[lane // CHEB]
-    out[1] = nodes[lane % CHEB]
+    point = lane & (RANK - 1)
+    which = point >> 3 if dim == 0 else point & 7
+    out = jnp.full(lane.shape, float(nodes[0]), F32)
+    for k in range(1, CHEB):
+        out = jnp.where(which == k, float(nodes[k]), out)
     return out
 
 
@@ -88,7 +90,7 @@
     return out
 
 
-def dim_tables(j, after, index, dim, nodes_ref):
+def dim_tables(j, after, index, dim):
     row = lax.broadcasted_iota(jnp.int32, (16, LANES), 0)
     lane = lax.broadcasted_iota(jnp.int32, (16, LANES), 1)
     half = (lane >= RANK).astype(jnp.int32)
@@ -96,7 +98,7 @@
         g = row * 16 + half * 8 + index if after else index * 32 + half * 16 + row
     else:
         g = row * 16 + index if after else index * 16 + row
-    z = jnp.broadcast_to(nodes_ref[dim : dim + 1, :], (16, LANES))
+    z = node_values(lane, dim)
     b = g >> j
     p = reversed_bits(g & ((1 << j) - 1), j)
     level = START + j
@@ -123,9 +125,9 @@
         ref[dim, k] = value
 
 
-def fill_phases(j, after, index_one, index_two, nodes_ref, tab_ref, store):
-    store_tables(tab_ref, 0, dim_tables(j, after, index_one, 0, nodes_ref))
-    store_tables(tab_ref, 1, dim_tables(j, after, index_two, 1, nodes_ref))
+def fill_phases(j, after, index_one, index_two, tab_ref, store):
+    store_tables(tab_ref, 0, dim_tables(j, after, index_one, 0))
+    store_tables(tab_ref, 1, dim_tables(j, after, index_two, 1))
 
     @pl.loop(0, 16)
     def _(i1):
@@ -158,13 +160,13 @@
     return pl.ds(pl.multiple_of((i1 * 4 + s) * 16 + 8 * h, 8), 8)
 
 
-def fill_final(index_one, index_two, nodes_ref, tab_ref, store):
+def fill_final(index_one, index_two, tab_ref, store):
     row = lax.broadcasted_iota(jnp.int32, (16, LANES), 0)
     lane = lax.broadcasted_iota(jnp.int32, (16, LANES), 1)
     half = (lane >= RANK).astype(jnp.int32)
     for dim in range(2):
         g = row * 16 + half * 8 + index_one if dim == 0 else row * 16 + index_two
-        z = jnp.broadcast_to(nodes_ref[dim : dim + 1, :], (16, LANES))
+        z = node_values(lane, dim)
         p = 2 * reversed_bits(g, LEVELS) + 1
         level = START + LEVELS
         wave = (-GRID / 2.0 + 0.5 * 2.0**level) + 2.0**level * z
@@ -200,64 +202,64 @@
     return jnp.where(row < 4, -1.0, 1.0).astype(F32)
 
 
-def level(bit, place, load, cos_of, sin_of, lhs_ref, w_ref, emit):
+def level(bit, place, load, cos_of, sin_of, lhs_refs, w_ref, emit, beside=None):
     signs = turn_signs()
 
-    @pl.loop(0, 8)
-    def _(r1):
-        for r2 in range(8):
-            for c in range(4):
-                i1 = insert(r1, bit, c >> 1)
-                i2 = insert(r2, bit, c & 1)
-                value = load(place(i1, i2))
-                turned = pltpu.roll(value, 4, 0) * signs
-                for s1 in range(2):
-                    parts = []
-                    for s2 in range(2):
-                        row = (i1 * 4 + (2 * s1 + s2)) * 16 + i2
-                        cos = cos_of(row)
-                        sin = sin_of(row)
-                        parts.append(value * cos + turned * sin)
-                    both = jnp.concatenate(parts, axis=0)
-                    high = both.astype(BF16)
-                    low = (both - high.astype(F32)).astype(BF16)
-                    start = pl.multiple_of(r1 * 256 + (r2 * 2 + s1) * 16, 16)
-                    lhs_ref[pl.ds(start, 16), 256 * c : 256 * c + 128] = high
-                    lhs_ref[pl.ds(start, 16), 256 * c + 128 : 256 * c + 256] = low
-
-    @pl.loop(0, 4)
-    def _(block):
-        y = jnp.dot(
-            lhs_ref[pl.ds(pl.multiple_of(block * 512, 512), 512), :],
-            w_ref[...],
-            preferred_element_type=F32,
-        )
+    def build(chunk, lhs_ref):
+        for q in range(SPAN):
+            r1 = chunk * SPAN + q
+            for r2 in range(8):
+                for c in range(4):
+                    i1 = insert(r1, bit, c >> 1)
+                    i2 = insert(r2, bit, c & 1)
+                    value = load(place(i1, i2))
+                    turned = pltpu.roll(value, 4, 0) * signs
+                    for s1 in range(2):
+                        parts = []
+                        for s2 in range(2):
+                            row = (i1 * 4 + (2 * s1 + s2)) * 16 + i2
+                            parts.append(value * cos_of(row) + turned * sin_of(row))
+                        both = jnp.concatenate(parts, axis=0)
+                        high = both.astype(BF16)
+                        low = (both - high.astype(F32)).astype(BF16)
+                        start = q * 256 + (r2 * 2 + s1) * 16
+                        lhs_ref[start : start + 16, 256 * c : 256 * c + 128] = high
+                        lhs_ref[start : start + 16, 256 * c + 128 : 256 * c + 256] = low
+
+    def multiply(chunk, lhs_ref):
+        y = jnp.dot(lhs_ref[...], w_ref[...], preferred_element_type=F32)
         y = y[:, :LANES] + y[:, LANES:]
-        for q in range(2):
-            r1 = block * 2 + q
+        for q in range(SPAN):
             for r2 in range(8):
                 base = (q * 8 + r2) * 32
                 new = [y[base + 8 * s : base + 8 * s + 8] for s in range(4)]
-                emit(r1, r2, new)
-
-
-def before_kernel(x_ref, w_ref, nodes_ref, out_ref, d0, d1, cos_ref, sin_ref, tab_ref, lhs_ref):
+                emit(chunk * SPAN + q, r2, new)
+
+    chunks = 8 // SPAN
+    first, second = lhs_refs
+    build(0, first)
+
+    @pl.loop(0, chunks // 2 - 1)
+    def _(k):
+        multiply(2 * k, first)
+        build(2 * k + 1, second)
+        multiply(2 * k + 1, second)
+        build(2 * k + 2, first)
+
+    multiply(chunks - 2, first)
+    build(chunks - 1, second)
+    multiply(chunks - 1, second)
+
+
+def before_kernel(x_hbm, w_hbm, out_ref, x_ref, w_ref, d0, d1, cos_ref, sin_ref, tab_ref, lhs0, lhs1, sems):
+    copy_x = pltpu.make_async_copy(x_hbm, x_ref, sems.at[0])
+    copy_w = pltpu.make_async_copy(w_hbm, w_ref, sems.at[1])
+    copy_x.start()
+    copy_w.start()
     index_one = lax.axis_index("sx")
     index_two = lax.axis_index("sy")
     lower = lax.broadcasted_iota(jnp.int32, (8, LANES), 1) < RANK
 
-    @pl.loop(0, 16)
-    def _(i1):
-        for part in range(2):
-            for h in range(2):
-                for pair in range(2):
-                    cols = slice(pair * LANES, (pair + 1) * LANES)
-                    a = x_ref[part, pl.ds(i1, 1), 8 * h : 8 * h + 8, cols].reshape(8, LANES)
-                    b = x_ref[part, pl.ds(i1 + 16, 1), 8 * h : 8 * h + 8, cols].reshape(8, LANES)
-                    start = (i1 * 16 + 8 * h) * 8 + part * 4 + 2 * pair
-                    d0[pl.ds(start, 8, stride=8), :] = jnp.where(lower, a, pltpu.roll(b, RANK, 1))
-                    d0[pl.ds(start + 1, 8, stride=8), :] = jnp.where(lower, pltpu.roll(a, RANK, 1), b)
-
     def place(i1, i2):
         return i1 * 16 + i2
 
@@ -268,7 +270,23 @@
             cos_ref[phase_rows(i1, s, h), :] = cos
             sin_ref[phase_rows(i1, s, h), :] = sin
 
-        fill_phases(j, False, index_one, index_two, nodes_ref, tab_ref, store)
+        fill_phases(j, False, index_one, index_two, tab_ref, store)
+        if j == 0:
+            copy_x.wait()
+
+            @pl.loop(0, 16)
+            def _(i1):
+                for part in range(2):
+                    for h in range(2):
+                        for pair in range(2):
+                            cols = slice(pair * LANES, (pair + 1) * LANES)
+                            a = x_ref[part, pl.ds(i1, 1), 8 * h : 8 * h + 8, cols].reshape(8, LANES)
+                            b = x_ref[part, pl.ds(i1 + 16, 1), 8 * h : 8 * h + 8, cols].reshape(8, LANES)
+                            start = (i1 * 16 + 8 * h) * 8 + part * 4 + 2 * pair
+                            d0[pl.ds(start, 8, stride=8), :] = jnp.where(lower, a, pltpu.roll(b, RANK, 1))
+                            d0[pl.ds(start + 1, 8, stride=8), :] = jnp.where(lower, pltpu.roll(a, RANK, 1), b)
+
+            copy_w.wait()
         source, target = refs[j % 2], refs[(j + 1) % 2]
 
         def load(pos):
@@ -294,13 +312,13 @@
             load,
             lambda row: cos_ref[pl.ds(row, 1), :],
             lambda row: sin_ref[pl.ds(row, 1), :],
-            lhs_ref,
+            (lhs0, lhs1),
             w_ref,
             emit,
         )
 
 
-def phases_kernel(nodes_ref, cos_ref, sin_ref, cosf_ref, sinf_ref, tab_ref):
+def phases_kernel(cos_ref, sin_ref, cosf_ref, sinf_ref, tab_ref):
     index_one = lax.axis_index("sx")
     index_two = lax.axis_index("sy")
     for step in range(LEVELS - HALF):
@@ -309,23 +327,44 @@
             cos_ref[step, phase_rows(i1, s, h), :] = cos
             sin_ref[step, phase_rows(i1, s, h), :] = sin
 
-        fill_phases(HALF + step, True, index_one, index_two, nodes_ref, tab_ref, store)
+        fill_phases(HALF + step, True, index_one, index_two, tab_ref, store)
 
     def store_final(i1, h, cos, sin):
         rows = pl.ds(pl.multiple_of(i1 * 16 + 8 * h, 8), 8)
         cosf_ref[rows, :] = cos
         sinf_ref[rows, :] = sin
 
-    fill_final(index_one, index_two, nodes_ref, tab_ref, store_final)
-
-
-def after_kernel(x_ref, w_ref, cos_ref, sin_ref, cosf_ref, sinf_ref, out_ref, d0, d1, lhs_ref):
+    fill_final(index_one, index_two, tab_ref, store_final)
+
+
+def after_kernel(x_hbm, w_hbm, cos_hbm, sin_hbm, cosf_hbm, sinf_hbm, out_ref, *scratch):
+    x_ref, w_ref, cos_ref, sin_ref, cosf_ref, sinf_ref, d0, d1, lhs0, lhs1, sems = scratch
+    steps = LEVELS - HALF
+    copy_w = pltpu.make_async_copy(w_hbm, w_ref, sems.at[2 * steps])
+    copies = [
+        (
+            pltpu.make_async_copy(cos_hbm.at[k], cos_ref.at[k], sems.at[2 * k]),
+            pltpu.make_async_copy(sin_hbm.at[k], sin_ref.at[k], sems.at[2 * k + 1]),
+        )
+        for k in range(steps)
+    ]
+    copies[-1] += (
+        pltpu.make_async_copy(cosf_hbm, cosf_ref, sems.at[2 * steps + 1]),
+        pltpu.make_async_copy(sinf_hbm, sinf_ref, sems.at[2 * steps + 2]),
+    )
+    copies[0] += (copy_w, pltpu.make_async_copy(x_hbm, x_ref, sems.at[2 * steps + 3]))
+    for group in copies:
+        for copy in group:
+            copy.start()
+
     def place(i1, i2):
         return (i1 >> 1) * 32 + i2 * 2 + (i1 & 1)
 
     signs = turn_signs()
     refs = (x_ref, d0, d1, d0, out_ref)
     for step in range(LEVELS - HALF):
+        for copy in copies[step]:
+            copy.wait()
         source, target = refs[step], refs[step + 1]
 
         def load(pos):
@@ -347,7 +386,7 @@
             load,
             lambda row: cos_ref[step, pl.ds(row, 1), :],
             lambda row: sin_ref[step, pl.ds(row, 1), :],
-            lhs_ref,
+            (lhs0, lhs1),
             w_ref,
             emit,
         )
@@ -374,28 +413,40 @@
 
 
 VMEM = pl.BlockSpec(memory_space=pltpu.VMEM)
+ANY = pl.BlockSpec(memory_space=pl.ANY)
 ROWS = 2048
 
 
 def local(weights):
     w = jnp.asarray(mixing_weights())
-    nodes = jnp.asarray(node_lanes())
     shape = jax.ShapeDtypeStruct((ROWS, LANES), F32)
     values = pltpu.VMEM((ROWS, LANES), F32)
     table = pltpu.VMEM((2, 6, 16, LANES), F32)
-    lhs = pltpu.VMEM((2048, 1024), BF16)
+    lhs = pltpu.VMEM((256 * SPAN, 1024), BF16)
+    mixing = pltpu.VMEM((1024, 2 * LANES), BF16)
     cost = functools.partial(pl.CostEstimate, transcendentals=0)
 
     before = pl.pallas_call(
         before_kernel,
         out_shape=shape,
-        in_specs=[VMEM] * 3,
+        in_specs=[ANY, ANY],
         out_specs=VMEM,
-        scratch_shapes=[values, values, pltpu.VMEM((1024, LANES), F32), pltpu.VMEM((1024, LANES), F32), table, lhs],
-        compiler_params=pltpu.CompilerParams(vmem_limit_bytes=24 * MIB),
+        scratch_shapes=[
+            pltpu.VMEM(weights.shape, F32),
+            mixing,
+            values,
+            values,
+            pltpu.VMEM((1024, LANES), F32),
+            pltpu.VMEM((1024, LANES), F32),
+            table,
+            lhs,
+            lhs,
+            pltpu.SemaphoreType.DMA((2,)),
+        ],
+        compiler_params=pltpu.CompilerParams(vmem_limit_bytes=59 * MIB),
         cost_estimate=cost(flops=4 * 2**31, bytes_accessed=3 * MIB),
         name="before",
-    )(weights, w, nodes)
+    )(weights, w)
 
     moved = lax.all_to_all(before.reshape(128, 16, LANES), ("sx", "sy"), 0, 0, tiled=True)
 
@@ -404,21 +455,33 @@
     phases = pl.pallas_call(
         phases_kernel,
         out_shape=(phase, phase, last, last),
-        in_specs=[VMEM],
+        in_specs=[],
         out_specs=(VMEM,) * 4,
         scratch_shapes=[table],
         compiler_params=pltpu.CompilerParams(vmem_limit_bytes=24 * MIB),
         cost_estimate=cost(flops=2**33, bytes_accessed=5 * MIB),
         name="phases",
-    )(nodes)
+    )()
 
     after = pl.pallas_call(
         after_kernel,
         out_shape=shape,
-        in_specs=[VMEM] * 6,
+        in_specs=[ANY] * 6,
         out_specs=VMEM,
-        scratch_shapes=[values, values, lhs],
-        compiler_params=pltpu.CompilerParams(vmem_limit_bytes=24 * MIB),
+        scratch_shapes=[
+            values,
+            mixing,
+            pltpu.VMEM(phase.shape, F32),
+            pltpu.VMEM(phase.shape, F32),
+            pltpu.VMEM(last.shape, F32),
+            pltpu.VMEM(last.shape, F32),
+            values,
+            values,
+            lhs,
+            lhs,
+            pltpu.SemaphoreType.DMA((2 * (LEVELS - HALF) + 4,)),
+        ],
+        compiler_params=pltpu.CompilerParams(vmem_limit_bytes=59 * MIB),
         cost_estimate=cost(flops=4 * 2**31, bytes_accessed=8 * MIB),
         name="after",
     )(moved.reshape(ROWS, LANES), w, *phases)

time: 90.4 us -> 77.7 us (0.86)
  Pallas kernels: 34.3 us -> 26 us
  local copies, waits for them, and re-layouts: 8.78 us -> 4.93 us
  waiting for transfers between devices: 12.3 us -> 11 us
    pallas_call x2, Pallas kernels: 28.5 us -> 20.3 us  [the longest x1 12.4 us: local(): pl.pallas_call(before_kernel, out_shape=shape, in_specs=[ANY, ANY], out_s...]
    unnamed x18 -> x10, local copies, waits for them, and re-layouts: 8.78 us -> 4.93 us
    all_to_all x1, waiting for transfers between devices: 12.3 us -> 11 us  [local(): lax.all_to_all(before.reshape(128, 16, LANES), ('sx', 'sy'), 0, 0, tiled=...]
  transfers between devices with their start and end apart: 1 -> 1, of which waited for: 1 -> 1; matrix products, arithmetic and copies ran while one was open for 0% -> 0% of each run, Pallas kernels for 4% -> 5%
where the time goes in v1:
time: 77.7 us; the launch traced here: 77.5 us
  Pallas kernels  26 us (33%)
  blocking collectives  23.9 us (31%)
  starting transfers between devices  11.5 us (15%)
  waiting for transfers between devices  11 us (14%)
  local copies, waits for them, and re-layouts  4.93 us (6%)
    all_to_all x1, blocking collectives, local(): lax.all_to_all(after.reshape(128, 16, LANES), ('sx', 'sy'), 0, 0, tiled=T...  23.9 us
    pallas_call x1, Pallas kernels, local(): pl.pallas_call(before_kernel, out_shape=shape, in_specs=[ANY, ANY], out_s...  12.4 us
    all_to_all x1, starting transfers between devices, local(): lax.all_to_all(before.reshape(128, 16, LANES), ('sx', 'sy'), 0, 0, tiled=...  11.5 us
    all_to_all x1, waiting for transfers between devices, local(): lax.all_to_all(before.reshape(128, 16, LANES), ('sx', 'sy'), 0, 0, tiled=...  11 us
    pallas_call x1, Pallas kernels, local(): pl.pallas_call(after_kernel, out_shape=shape, in_specs=[ANY] * 6, out_spe...  7.9 us
    unnamed x10, local copies, waits for them, and re-layouts  4.93 us
    pallas_call x1, Pallas kernels, local(): pl.pallas_call(phases_kernel, out_shape=(phase, phase, last, last), in_sp...  3.91 us
    pallas_call x1, Pallas kernels, local(): pl.pallas_call(order_kernel, out_shape=jax.ShapeDtypeStruct(weights.shape...  1.82 us
  transfers between devices with their start and end apart: 1, of which 1 were waited for; matrix products, arithmetic and copies ran while one was open for 0% of the time, Pallas kernels for 5%

profile of v1, /device:TPU:1, one launch (start us, length us, event | category | flops | bytes accessed | tf_op | source)
XLA Modules:
  0.0 77.5 jit_solution(15671189140708038774)
XLA Ops:
  0.0 12.4 %before.1 = f32[2048,128]{1,0:T(8,128)} custom-call(f32[2,32,16,256]{3,2,1,0:T(8,128)} %x_hbm.1, bf16[1024,256]{1,0:T(8,128)(2,1)} %constant.2.clone.w_hbm), custom_call_target="tpu_custom_call" | custom-call | flops 8589934592 | bytes 3145728 | tf_op jit(solution)/shard_map/before/pallas_call | solution.py:429
  12.4 11.5 %all-to-all-start = ((f32[128,16,128]{2,1,0:T(8,128)}), f32[128,16,128]{2,1,0:T(8,128)S(1)}, u32[]{:S(2)}, u32[]{:S(2)}) async-start(f32[128,16,128]{2,1,0:T(8,128)} %bitcast.6), calls=%async_computation | async-start | bytes 2097152 | tf_op jit(solution)/shard_map/all_to_all | solution.py:451
  23.9 3.9 %phases.1 = (f32[4,1024,128]{2,1,0:T(8,128)S(1)}, f32[4,1024,128]{2,1,0:T(8,128)S(1)}, f32[256,128]{1,0:T(8,128)S(1)}, f32[256,128]{1,0:T(8,128)S(1)}) custom-call(), custom_call_target="tpu_custom_call" | custom-call | flops 8589934592 | bytes 5242880 | tf_op jit(solution)/shard_map/phases/pallas_call | solution.py:455
  27.8 0.0 copy-start
  27.9 1.3 %copy-done = f32[4,1024,128]{2,1,0:T(8,128)} copy-done((f32[4,1024,128]{2,1,0:T(8,128)}, f32[4,1024,128]{2,1,0:T(8,128)S(1)}, u32[]{:S(2)}) %copy-start) | copy-done | bytes 2097176
  29.2 0.0 copy-start.1
  29.2 1.3 %copy-done.1 = f32[4,1024,128]{2,1,0:T(8,128)} copy-done((f32[4,1024,128]{2,1,0:T(8,128)}, f32[4,1024,128]{2,1,0:T(8,128)S(1)}, u32[]{:S(2)}) %copy-start.1) | copy-done | bytes 2097176
  30.5 0.0 copy-start.2
  30.5 0.6 copy-done.2
  31.2 0.0 copy-start.3
  31.2 0.7 copy-done.3
  31.8 11.0 %all-to-all-done = f32[128,16,128]{2,1,0:T(8,128)S(1)} async-done(((f32[128,16,128]{2,1,0:T(8,128)}), f32[128,16,128]{2,1,0:T(8,128)S(1)}, u32[]{:S(2)}, u32[]{:S(2)}) %all-to-all-start) | async-done | bytes 1048608 | tf_op jit(solution)/shard_map/all_to_all | solution.py:451
  42.8 0.0 copy-start.4
  42.8 1.0 %copy-done.4 = f32[128,16,128]{2,1,0:T(8,128)} copy-done((f32[128,16,128]{2,1,0:T(8,128)}, f32[128,16,128]{2,1,0:T(8,128)S(1)}, u32[]{:S(2)}) %copy-start.4) | copy-done | bytes 1048600
  43.8 7.9 %after.1 = f32[2048,128]{1,0:T(8,128)} custom-call(f32[2048,128]{1,0:T(8,128)} %bitcast.5, bf16[1024,256]{1,0:T(8,128)(2,1)} %constant.2.clone.w_hbm, f32[4,1024,128]{2,1,0:T(8,128)} %copy-done, f32[4,1024,128]{2,1,0:T(8,128)} %copy-done.1, f32[256,128]{1,0:T(8,128)} %copy-done.2, f32[256,128]{1,0:T(8,128)} %copy-done.3), custom_call_target="tpu_custom_call" | custom-call | flops 8589934592 | bytes 8388608 | tf_op jit(solution)/shard_map/after/pallas_call | solution.py:466
  51.7 23.9 %all_to_all.10 = f32[128,16,128]{2,1,0:T(8,128)S(1)} all-to-all(f32[128,16,128]{2,1,0:T(8,128)} %bitcast.7), channel_id=1, replica_groups=mesh['sx'=8,'sy'=16] {'sx','sy'}, dimensions={0} | all-to-all | bytes 2097152 | tf_op jit(solution)/shard_map/all_to_all | solution.py:489
  75.6 1.8 %order.1 = f32[2,32,16,256]{3,2,1,0:T(8,128)} custom-call(f32[2048,128]{1,0:T(8,128)S(1)} %bitcast.4), custom_call_target="tpu_custom_call" | custom-call | flops 1048576 | bytes 2097152 | tf_op jit(solution)/shard_map/order/pallas_call | solution.py:491
Async XLA Ops:
  12.4 30.4 %all-to-all-start = ((f32[128,16,128]{2,1,0:T(8,128)}), f32[128,16,128]{2,1,0:T(8,128)S(1)}, u32[]{:S(2)}, u32[]{:S(2)}) async-start(f32[128,16,128]{2,1,0:T(8,128)} %bitcast.6), calls=%async_computation | async-start | bytes 2097152 | tf_op jit(solution)/shard_map/all_to_all | solution.py:451
  27.8 1.3 %copy-start = (f32[4,1024,128]{2,1,0:T(8,128)}, f32[4,1024,128]{2,1,0:T(8,128)S(1)}, u32[]{:S(2)}) copy-start(f32[4,1024,128]{2,1,0:T(8,128)S(1)} %get-tuple-element.9.cos_hbm) | copy-start | bytes 6291460
  29.2 1.3 %copy-start.1 = (f32[4,1024,128]{2,1,0:T(8,128)}, f32[4,1024,128]{2,1,0:T(8,128)S(1)}, u32[]{:S(2)}) copy-start(f32[4,1024,128]{2,1,0:T(8,128)S(1)} %get-tuple-element.10.sin_hbm) | copy-start | bytes 6291460
  30.5 0.7 copy-start.2
  31.2 0.7 copy-start.3
  42.8 1.0 %copy-start.4 = (f32[128,16,128]{2,1,0:T(8,128)}, f32[128,16,128]{2,1,0:T(8,128)S(1)}, u32[]{:S(2)}) copy-start(f32[128,16,128]{2,1,0:T(8,128)S(1)} %all-to-all-done) | copy-start | bytes 3145732

commit v2 on v1

v2 whole, which is shorter than its diff:
```python
import functools
import math

import jax
import jax.numpy as jnp
import ml_dtypes
import numpy as np
from jax import lax
from jax.experimental import pallas as pl
from jax.experimental.pallas import tpu as pltpu
from jax.sharding import PartitionSpec as P

CHEB = 8
RANK = 64
GRID = 4096
LEVELS = 8
START = 2
HALF = 4
LANES = 2 * RANK
F32 = jnp.float32
BF16 = jnp.bfloat16
MIB = 1 << 20
STEP_ROWS = 1024
PHASE_ROWS = (LEVELS - HALF) * STEP_ROWS + 256

SIN_TERMS = (6.283184916, -41.34158923, 81.59994333, -76.61447253, 41.34288235, -12.47124353)
COS_TERMS = (0.9999999891, -19.7392045, 64.93911746, -85.45013953, 60.16763095, -25.96759925, 6.528658158)


def lagrange_tables(node_count):
    cheb_nodes = 0.5 * np.cos((2.0 * np.arange(node_count) + 1.0) * math.pi / (2.0 * node_count))
    single = np.ones((2, node_count, node_count))
    for child_bit in range(2):
        for source in range(node_count):
            location = (child_bit - 0.5) / 2.0 + cheb_nodes[source] / 2.0
            for target in range(node_count):
                for another in range(node_count):
                    if another != target:
                        single[child_bit, source, target] *= (location - cheb_nodes[another]) / (
                            cheb_nodes[target] - cheb_nodes[another]
                        )
    paired = single[:, None, :, None, :, None] * single[None, :, None, :, None, :]
    paired = paired.reshape(2, 2, node_count * node_count, node_count * node_count)
    return (cheb_nodes, paired)


def mixing_weights():
    table = lagrange_tables(CHEB)[1].astype(np.float32).reshape(4, RANK, RANK)
    high = table.astype(ml_dtypes.bfloat16)
    low = (table - high.astype(np.float32)).astype(ml_dtypes.bfloat16)
    out = np.zeros((4, 2, LANES, 2, LANES), ml_dtypes.bfloat16)
    for half in range(2):
        part = slice(half * RANK, (half + 1) * RANK)
        for split in range(2):
            out[:, split, part, 0, part] = high
            out[:, split, part, 1, part] = low
    return out.reshape(4 * 2 * LANES, 2 * LANES)


def node_values(lane, dim):
    nodes = lagrange_tables(CHEB)[0].astype(np.float32)
    point = lane & (RANK - 1)
    which = point >> 3 if dim == 0 else point & 7
    out = jnp.full(lane.shape, float(nodes[0]), F32)
    for k in range(1, CHEB):
        out = jnp.where(which == k, float(nodes[k]), out)
    return out


def poly(terms, u):
    acc = terms[-1] * u + terms[-2]
    for term in terms[-3::-1]:
        acc = acc * u + term
    return acc


def sin_turns(f):
    return f * poly(SIN_TERMS, f * f)


def cos_sin(turns):
    f = turns - jnp.round(turns)
    u = f * f
    return poly(COS_TERMS, u), f * poly(SIN_TERMS, u)


def reversed_bits(values, count):
    out = jnp.zeros_like(values)
    for bit in range(count):
        out = out + (((values >> bit) & 1) << (count - 1 - bit))
    return out


def dim_tables(j, after, index, dim):
    row = lax.broadcasted_iota(jnp.int32, (16, LANES), 0)
    lane = lax.broadcasted_iota(jnp.int32, (16, LANES), 1)
    half = (lane >= RANK).astype(jnp.int32)
    if dim == 0:
        g = row * 16 + half * 8 + index if after else index * 32 + half * 16 + row
    else:
        g = row * 16 + index if after else index * 16 + row
    z = node_values(lane, dim)
    b = g >> j
    p = reversed_bits(g & ((1 << j) - 1), j)
    level = START + j
    width = 2.0**level
    wave = (-GRID / 2.0 + (b.astype(F32) + 0.5) * width) + width * z
    odd = ((2 * b + 1) & 7).astype(F32) * 0.125
    linear = odd + 0.25 * z
    p = p.astype(F32)
    parent = sin_turns((p + 0.5) * 0.5**level)
    new = [sin_turns((2.0 * p + (s + 0.5)) * 0.5 ** (level + 1)) for s in range(2)]
    if j == 0:
        lin = []
        for s in range(2):
            whole = (((2 * b + 1) * (2 * s + 1)) & 7).astype(F32) * 0.125
            lin.append(-(whole + ((2 * s + 1) * 0.25) * z))
    else:
        lin = [linear, -linear]
    return wave, lin, parent, new


def store_tables(ref, dim, tables):
    wave, lin, parent, new = tables
    for k, value in enumerate((wave, lin[0], lin[1], parent, new[0], new[1])):
        ref[dim, k] = value


def fill_tables(j, after, index_one, index_two, tab_ref):
    store_tables(tab_ref, 0, dim_tables(j, after, index_one, 0))
    store_tables(tab_ref, 1, dim_tables(j, after, index_two, 1))


def phases_at(i1, j, tab_ref, store):
    def one(k):
        return jnp.broadcast_to(tab_ref[0, k, pl.ds(i1, 1), :], (8, LANES))

    wave1 = one(0)
    wave1 = wave1 * wave1
    lin1 = (one(1), one(2))
    par1, new1 = one(3) * 0.0625, (one(4) * 0.0625, one(5) * 0.0625)
    for h in range(2):

        def two(k):
            return tab_ref[1, k, 8 * h : 8 * h + 8, :]

        wave2 = two(0)
        radius = jnp.sqrt(wave1 + wave2 * wave2)
        lin2 = (two(1), two(2))
        par = par1 * two(3)
        for s1 in range(2):
            for s2 in range(2):
                new = new1[s1] * two(4 + s2)
                bend = -(0.125 + new) if j == 0 else par - new
                turns = bend * radius + (lin1[s1] + lin2[s2])
                cos, sin = cos_sin(turns)
                store(i1, 2 * s1 + s2, h, cos, sin)


def fill_phases(j, after, index_one, index_two, tab_ref, store):
    fill_tables(j, after, index_one, index_two, tab_ref)

    @pl.loop(0, 16)
    def _(i1):
        phases_at(i1, j, tab_ref, store)


def phase_rows(i1, s, h):
    start = (i1 * 4 + s) * 16 + 8 * h
    return pl.ds(start if isinstance(start, int) else pl.multiple_of(start, 8), 8)


def fill_final(index_one, index_two, tab_ref, store):
    row = lax.broadcasted_iota(jnp.int32, (16, LANES), 0)
    lane = lax.broadcasted_iota(jnp.int32, (16, LANES), 1)
    half = (lane >= RANK).astype(jnp.int32)
    for dim in range(2):
        g = row * 16 + half * 8 + index_one if dim == 0 else row * 16 + index_two
        z = node_values(lane, dim)
        p = 2 * reversed_bits(g, LEVELS) + 1
        level = START + LEVELS
        wave = (-GRID / 2.0 + 0.5 * 2.0**level) + 2.0**level * z
        whole = ((-3 * p) & 3).astype(F32) * 0.25
        tab_ref[dim, 0] = wave
        tab_ref[dim, 1] = whole + (p.astype(F32) * 0.5) * z
        tab_ref[dim, 2] = sin_turns(p.astype(F32) * 0.5 ** (level + 1))

    @pl.loop(0, 16)
    def _(i1):
        def one(k):
            return jnp.broadcast_to(tab_ref[0, k, pl.ds(i1, 1), :], (8, LANES))

        wave1, lin1, sin1 = one(0), one(1), one(2) * 0.0625
        for h in range(2):
            rows = slice(8 * h, 8 * h + 8)
            wave2 = tab_ref[1, 0, rows, :]
            radius = jnp.sqrt(wave1 * wave1 + wave2 * wave2)
            bend = 0.125 + sin1 * tab_ref[1, 2, rows, :]
            turns = bend * radius + (lin1 + tab_ref[1, 1, rows, :])
            turns = turns - jnp.round(turns)
            cos, sin = cos_sin(turns)
            store(i1, h, cos, sin)


def insert(rest, bit, value):
    low = rest & ((1 << bit) - 1)
    return ((rest >> bit) << (bit + 1)) + (value << bit) + low


def turn_signs():
    row = lax.broadcasted_iota(jnp.int32, (8, LANES), 0)
    return jnp.where(row < 4, -1.0, 1.0).astype(F32)


QUARTERS = ((3, 2), (3, 2), (3, 0), (0, 1))


def quarter_bases(step, quarter):
    slow, fast = QUARTERS[step]
    rest = 6 - step - slow - fast
    base = ((quarter >> 1) << slow) + ((quarter & 1) << fast)
    return (base, base + (1 << rest))


def levels(place, load, cos_of, sin_of, lhs_refs, w_ref, emit, before_level, beside):
    signs = turn_signs()

    def build(step, quarter, lhs_ref):
        for q, base in enumerate(quarter_bases(step, quarter)):
            for r2 in range(8):
                for c in range(4):
                    i1 = base + ((c >> 1) << step)
                    i2 = insert(r2, step, c & 1)
                    value = load(step, place(i1, i2))
                    turned = pltpu.roll(value, 4, 0) * signs
                    for s1 in range(2):
                        parts = []
                        for s2 in range(2):
                            row = (i1 * 4 + (2 * s1 + s2)) * 16 + i2
                            parts.append(value * cos_of(step, row) + turned * sin_of(step, row))
                        both = jnp.concatenate(parts, axis=0)
                        high = both.astype(BF16)
                        low = (both - high.astype(F32)).astype(BF16)
                        start = q * 256 + (r2 * 2 + s1) * 16
                        lhs_ref[start : start + 16, 256 * c : 256 * c + 128] = high
                        lhs_ref[start : start + 16, 256 * c + 128 : 256 * c + 256] = low

    def multiply(step, quarter, lhs_ref):
        y = jnp.dot(lhs_ref[...], w_ref[...], preferred_element_type=F32)
        y = y[:, :LANES] + y[:, LANES:]
        for q, base in enumerate(quarter_bases(step, quarter)):
            for r2 in range(8):
                rows = (q * 8 + r2) * 32
                new = [y[rows + 8 * s : rows + 8 * s + 8] for s in range(4)]
                emit(step, base, r2, new)

    def stage(n):
        if n < 16:
            build(n // 4, n % 4, lhs_refs[n % 2])
        if n > 0:
            multiply((n - 1) // 4, (n - 1) % 4, lhs_refs[(n - 1) % 2])
        if n < 16:
            beside(n // 4, n % 4)

    always = lax.axis_index("sx") >= 0
    for n in range(17):
        if n % 4 == 0 and n < 16:
            before_level(n // 4)
        pl.when(always)(functools.partial(stage, n))


def before_kernel(x_hbm, w_hbm, out_ref, x_ref, w_ref, d0, d1, cos0, sin0, cos1, sin1, tab_ref, lhs0, lhs1, sems):
    copy_x = pltpu.make_async_copy(x_hbm, x_ref, sems.at[0])
    copy_w = pltpu.make_async_copy(w_hbm, w_ref, sems.at[1])
    copy_x.start()
    copy_w.start()
    index_one = lax.axis_index("sx")
    index_two = lax.axis_index("sy")
    lower = lax.broadcasted_iota(jnp.int32, (8, LANES), 1) < RANK
    cos_refs, sin_refs = (cos0, cos1), (sin0, sin1)
    values = (d0, d1)

    def store_in(step):
        def store(i1, s, h, cos, sin):
            cos_refs[step % 2][phase_rows(i1, s, h), :] = cos
            sin_refs[step % 2][phase_rows(i1, s, h), :] = sin

        return store

    for step in range(HALF):
        fill_tables(step, False, index_one, index_two, tab_ref.at[step])

    @pl.loop(0, 16)
    def _(i1):
        phases_at(i1, 0, tab_ref.at[0], store_in(0))

    copy_x.wait()

    @pl.loop(0, 16)
    def _(i1):
        for part in range(2):
            for h in range(2):
                for pair in range(2):
                    cols = slice(pair * LANES, (pair + 1) * LANES)
                    a = x_ref[part, pl.ds(i1, 1), 8 * h : 8 * h + 8, cols].reshape(8, LANES)
                    b = x_ref[part, pl.ds(i1 + 16, 1), 8 * h : 8 * h + 8, cols].reshape(8, LANES)
                    start = (i1 * 16 + 8 * h) * 8 + part * 4 + 2 * pair
                    d0[pl.ds(start, 8, stride=8), :] = jnp.where(lower, a, pltpu.roll(b, RANK, 1))
                    d0[pl.ds(start + 1, 8, stride=8), :] = jnp.where(lower, pltpu.roll(a, RANK, 1), b)

    copy_w.wait()

    def place(i1, i2):
        return i1 * 16 + i2

    def load(step, pos):
        return values[step % 2][pos * 8 : pos * 8 + 8, :]

    def emit(step, base, r2, new):
        if step < HALF - 1:
            for s in range(4):
                pos = place(base + ((s >> 1) << step), insert(r2, step, s & 1))
                values[(step + 1) % 2][pos * 8 : pos * 8 + 8, :] = new[s]
        else:
            for s2 in range(2):
                a, b = new[s2], new[2 + s2]
                row = (base * 16 + insert(r2, step, s2)) * 16
                out_ref[row : row + 8, :] = jnp.where(lower, a, pltpu.roll(b, RANK, 1))
                out_ref[row + 8 : row + 16, :] = jnp.where(lower, pltpu.roll(a, RANK, 1), b)

    def beside(step, quarter):
        if step < HALF - 1:
            for i1 in range(4 * quarter, 4 * quarter + 4):
                phases_at(i1, step + 1, tab_ref.at[step + 1], store_in(step + 1))

    levels(
        place,
        load,
        lambda step, row: cos_refs[step % 2][row : row + 1, :],
        lambda step, row: sin_refs[step % 2][row : row + 1, :],
        (lhs0, lhs1),
        w_ref,
        emit,
        lambda step: None,
        beside,
    )


def phases_kernel(out_ref, tab_ref):
    index_one = lax.axis_index("sx")
    index_two = lax.axis_index("sy")
    for step in range(LEVELS - HALF):

        def store(i1, s, h, cos, sin):
            rows = pl.ds(pl.multiple_of(step * STEP_ROWS + (i1 * 4 + s) * 16 + 8 * h, 8), 8)
            out_ref[0, rows, :] = cos
            out_ref[1, rows, :] = sin

        fill_phases(HALF + step, True, index_one, index_two, tab_ref, store)

    def store_final(i1, h, cos, sin):
        rows = pl.ds(pl.multiple_of((LEVELS - HALF) * STEP_ROWS + i1 * 16 + 8 * h, 8), 8)
        out_ref[0, rows, :] = cos
        out_ref[1, rows, :] = sin

    fill_final(index_one, index_two, tab_ref, store_final)


def after_kernel(x_ref, w_hbm, turns_hbm, out_ref, w_ref, turns_ref, d0, d1, lhs0, lhs1, sems):
    steps = LEVELS - HALF
    copies = []
    for k in range(steps):
        first = k * STEP_ROWS
        rows = pl.ds(first, STEP_ROWS if k < steps - 1 else PHASE_ROWS - first)
        copies.append([pltpu.make_async_copy(turns_hbm.at[:, rows], turns_ref.at[:, rows], sems.at[k])])
    copies[0].append(pltpu.make_async_copy(w_hbm, w_ref, sems.at[steps]))
    for group in copies:
        for copy in group:
            copy.start()
    signs = turn_signs()
    refs = (x_ref, d0, d1, d0, out_ref)

    def place(i1, i2):
        return (i1 >> 1) * 32 + i2 * 2 + (i1 & 1)

    def load(step, pos):
        return refs[step][pos * 8 : pos * 8 + 8, :]

    def emit(step, base, r2, new):
        for s in range(4):
            i1, i2 = base + ((s >> 1) << step), insert(r2, step, s & 1)
            value = new[s]
            if step == steps - 1:
                row = steps * STEP_ROWS + i1 * 16 + i2
                cos, sin = turns_ref[0, row : row + 1, :], turns_ref[1, row : row + 1, :]
                value = value * cos + (pltpu.roll(value, 4, 0) * signs) * sin
            pos = place(i1, i2) * 8
            refs[step + 1][pos : pos + 8, :] = value

    def before_level(step):
        for copy in copies[step]:
            copy.wait()

    levels(
        place,
        load,
        lambda step, row: turns_ref[0, step * STEP_ROWS + row : step * STEP_ROWS + row + 1, :],
        lambda step, row: turns_ref[1, step * STEP_ROWS + row : step * STEP_ROWS + row + 1, :],
        (lhs0, lhs1),
        w_ref,
        emit,
        before_level,
        lambda step, quarter: None,
    )


def order_kernel(x_ref, out_ref):
    lower = lax.broadcasted_iota(jnp.int32, (8, LANES), 1) < RANK
    part = pl.program_id(0)

    @pl.loop(0, 8)
    def _(sx):
        for b4 in range(2):
            for pair in range(2):
                cols = slice(pair * LANES, (pair + 1) * LANES)
                for h in range(2):
                    start = ((sx * 16 + 8 * h) * 2 + b4) * 8 + part * 4 + 2 * pair
                    a = x_ref[pl.ds(start, 8, stride=16), :]
                    b = x_ref[pl.ds(start + 1, 8, stride=16), :]
                    first = jnp.where(lower, a, pltpu.roll(b, RANK, 1))
                    second = jnp.where(lower, pltpu.roll(a, RANK, 1), b)
                    rows = slice(8 * h, 8 * h + 8)
                    out_ref[0, pl.ds(b4 * 16 + sx, 1), rows, cols] = first[None]
                    out_ref[0, pl.ds(b4 * 16 + 8 + sx, 1), rows, cols] = second[None]


VMEM = pl.BlockSpec(memory_space=pltpu.VMEM)
HBM = pl.BlockSpec(memory_space=pltpu.HBM)
ROWS = 2048


def local(weights):
    w = jnp.asarray(mixing_weights())
    shape = jax.ShapeDtypeStruct((ROWS, LANES), F32)
    values = pltpu.VMEM((ROWS, LANES), F32)
    table = pltpu.VMEM((2, 6, 16, LANES), F32)
    lhs = pltpu.VMEM((512, 1024), BF16)
    mixing = pltpu.VMEM((1024, 2 * LANES), BF16)
    cost = functools.partial(pl.CostEstimate, transcendentals=0)

    before = pl.pallas_call(
        before_kernel,
        out_shape=shape,
        in_specs=[HBM, HBM],
        out_specs=VMEM,
        scratch_shapes=[
            pltpu.VMEM(weights.shape, F32),
            mixing,
            values,
            values,
            *[pltpu.VMEM((1024, LANES), F32)] * 4,
            pltpu.VMEM((HALF, 2, 6, 16, LANES), F32),
            lhs,
            lhs,
            pltpu.SemaphoreType.DMA((2,)),
        ],
        compiler_params=pltpu.CompilerParams(vmem_limit_bytes=59 * MIB),
        cost_estimate=cost(flops=4 * 2**31, bytes_accessed=3 * MIB),
        name="before",
    )(weights, w)

    moved = lax.all_to_all(before.reshape(128, 16, LANES), ("sx", "sy"), 0, 0, tiled=True)

    phase = jax.ShapeDtypeStruct((2, PHASE_ROWS, LANES), F32)
    phases = pl.pallas_call(
        phases_kernel,
        out_shape=phase,
        in_specs=[],
        out_specs=VMEM,
        scratch_shapes=[table],
        compiler_params=pltpu.CompilerParams(vmem_limit_bytes=24 * MIB),
        cost_estimate=cost(flops=2**33, bytes_accessed=5 * MIB),
        name="phases",
    )()

    after = pl.pallas_call(
        after_kernel,
        out_shape=shape,
        in_specs=[VMEM, HBM, HBM],
        out_specs=VMEM,
        scratch_shapes=[
            mixing,
            pltpu.VMEM(phase.shape, F32),
            values,
            values,
            lhs,
            lhs,
            pltpu.SemaphoreType.DMA((LEVELS - HALF + 1,)),
        ],
        compiler_params=pltpu.CompilerParams(vmem_limit_bytes=59 * MIB),
        cost_estimate=cost(flops=4 * 2**31, bytes_accessed=8 * MIB),
        name="after",
    )(moved.reshape(ROWS, LANES), w, phases)

    moved = lax.all_to_all(after.reshape(128, 16, LANES), ("sx", "sy"), 0, 0, tiled=True)

    return pl.pallas_call(
        order_kernel,
        out_shape=jax.ShapeDtypeStruct(weights.shape, F32),
        grid=(2,),
        in_specs=[VMEM],
        out_specs=pl.BlockSpec((1, *weights.shape[1:]), lambda part: (part, 0, 0, 0)),
        compiler_params=pltpu.CompilerParams(vmem_limit_bytes=8 * MIB),
        cost_estimate=cost(flops=2**20, bytes_accessed=2 * MIB),
        name="order",
    )(moved.reshape(ROWS, LANES))


def solution(mesh):
    return jax.shard_map(
        local,
        mesh=mesh,
        in_specs=(P(None, "sx", "sy", None),),
        out_specs=P(None, "sx", "sy", None),
        check_vma=False,
    )
```

time: 77.7 us -> 77.8 us (level)
  waiting for transfers between devices: 11 us -> 13 us
  local copies, waits for them, and re-layouts: 4.93 us -> 2.99 us
    all_to_all x1, waiting for transfers between devices: 11 us -> 13 us  [local(): lax.all_to_all(before.reshape(128, 16, LANES), ('sx', 'sy'), 0, 0, tiled=...]
    unnamed x10 -> x4, local copies, waits for them, and re-layouts: 4.93 us -> 2.99 us
where the time goes in v2:
time: 77.8 us; the launch traced here: 77.5 us
  Pallas kernels  26.1 us (34%)
  blocking collectives  23.9 us (31%)
  waiting for transfers between devices  13 us (17%)
  starting transfers between devices  11.5 us (15%)
  local copies, waits for them, and re-layouts  2.99 us (4%)
    all_to_all x1, blocking collectives, local(): lax.all_to_all(after.reshape(128, 16, LANES), ('sx', 'sy'), 0, 0, tiled=T...  23.9 us
    all_to_all x1, waiting for transfers between devices, local(): lax.all_to_all(before.reshape(128, 16, LANES), ('sx', 'sy'), 0, 0, tiled=...  13 us
    all_to_all x1, starting transfers between devices, local(): lax.all_to_all(before.reshape(128, 16, LANES), ('sx', 'sy'), 0, 0, tiled=...  11.5 us
    pallas_call x1, Pallas kernels, local(): pl.pallas_call(before_kernel, out_shape=shape, in_specs=[HBM, HBM], out_s...  10.2 us
    pallas_call x1, Pallas kernels, local(): pl.pallas_call(after_kernel, out_shape=shape, in_specs=[VMEM, HBM, HBM],...  9.75 us
    pallas_call x1, Pallas kernels, local(): pl.pallas_call(phases_kernel, out_shape=phase, in_specs=[], out_specs=VME...  3.88 us
    unnamed x4, local copies, waits for them, and re-layouts  2.99 us
    pallas_call x1, Pallas kernels, local(): pl.pallas_call(order_kernel, out_shape=jax.ShapeDtypeStruct(weights.shape...  2.24 us
  transfers between devices with their start and end apart: 1, of which 1 were waited for; matrix products, arithmetic and copies ran while one was open for 0% of the time, Pallas kernels for 5%

profile of v2, /device:TPU:1, one launch (start us, length us, event | category | flops | bytes accessed | tf_op | source)
XLA Modules:
  0.0 77.5 jit_solution(5346738390298953153)
XLA Ops:
  0.0 10.2 %before.1 = f32[2048,128]{1,0:T(8,128)} custom-call(f32[2,32,16,256]{3,2,1,0:T(8,128)} %x_hbm.1, bf16[1024,256]{1,0:T(8,128)(2,1)} %constant.2.clone.w_hbm), custom_call_target="tpu_custom_call" | custom-call | flops 8589934592 | bytes 3145728 | tf_op jit(solution)/shard_map/before/pallas_call | solution.py:451
  10.2 11.5 %all-to-all-start = ((f32[128,16,128]{2,1,0:T(8,128)}), f32[128,16,128]{2,1,0:T(8,128)S(1)}, u32[]{:S(2)}, u32[]{:S(2)}) async-start(f32[128,16,128]{2,1,0:T(8,128)} %bitcast.6), calls=%async_computation | async-start | bytes 2097152 | tf_op jit(solution)/shard_map/all_to_all | solution.py:472
  21.7 3.9 %phases.1.turns_hbm = f32[2,4352,128]{2,1,0:T(8,128)S(1)} custom-call(), custom_call_target="tpu_custom_call" | custom-call | flops 8589934592 | bytes 5242880 | tf_op jit(solution)/shard_map/phases/pallas_call | solution.py:475
  25.6 0.0 copy-start
  25.6 2.0 %copy-done = f32[2,4352,128]{2,1,0:T(8,128)} copy-done((f32[2,4352,128]{2,1,0:T(8,128)}, f32[2,4352,128]{2,1,0:T(8,128)S(1)}, u32[]{:S(2)}) %copy-start) | copy-done | bytes 4456472
  27.6 13.0 %all-to-all-done = f32[128,16,128]{2,1,0:T(8,128)S(1)} async-done(((f32[128,16,128]{2,1,0:T(8,128)}), f32[128,16,128]{2,1,0:T(8,128)S(1)}, u32[]{:S(2)}, u32[]{:S(2)}) %all-to-all-start) | async-done | bytes 1048608 | tf_op jit(solution)/shard_map/all_to_all | solution.py:472
  40.6 0.0 copy-start.1
  40.6 1.0 %copy-done.1 = f32[128,16,128]{2,1,0:T(8,128)} copy-done((f32[128,16,128]{2,1,0:T(8,128)}, f32[128,16,128]{2,1,0:T(8,128)S(1)}, u32[]{:S(2)}) %copy-start.1) | copy-done | bytes 1048600
  41.6 9.8 %after.1 = f32[2048,128]{1,0:T(8,128)} custom-call(f32[2048,128]{1,0:T(8,128)} %bitcast.5, bf16[1024,256]{1,0:T(8,128)(2,1)} %constant.2.clone.w_hbm, f32[2,4352,128]{2,1,0:T(8,128)} %copy-done), custom_call_target="tpu_custom_call" | custom-call | flops 8589934592 | bytes 8388608 | tf_op jit(solution)/shard_map/after/pallas_call | solution.py:486
  51.4 23.9 %all_to_all.10 = f32[128,16,128]{2,1,0:T(8,128)S(1)} all-to-all(f32[128,16,128]{2,1,0:T(8,128)} %bitcast.7), channel_id=1, replica_groups=mesh['sx'=8,'sy'=16] {'sx','sy'}, dimensions={0} | all-to-all | bytes 2097152 | tf_op jit(solution)/shard_map/all_to_all | solution.py:505
  75.3 2.2 %order.1 = f32[2,32,16,256]{3,2,1,0:T(8,128)} custom-call(f32[2048,128]{1,0:T(8,128)S(1)} %bitcast.4), custom_call_target="tpu_custom_call" | custom-call | flops 1048576 | bytes 2097152 | tf_op jit(solution)/shard_map/order/pallas_call | solution.py:507
Async XLA Ops:
  10.2 30.4 %all-to-all-start = ((f32[128,16,128]{2,1,0:T(8,128)}), f32[128,16,128]{2,1,0:T(8,128)S(1)}, u32[]{:S(2)}, u32[]{:S(2)}) async-start(f32[128,16,128]{2,1,0:T(8,128)} %bitcast.6), calls=%async_computation | async-start | bytes 2097152 | tf_op jit(solution)/shard_map/all_to_all | solution.py:472
  25.6 2.0 %copy-start = (f32[2,4352,128]{2,1,0:T(8,128)}, f32[2,4352,128]{2,1,0:T(8,128)S(1)}, u32[]{:S(2)}) copy-start(f32[2,4352,128]{2,1,0:T(8,128)S(1)} %phases.1.turns_hbm) | copy-start | bytes 13369348
  40.6 1.0 %copy-start.1 = (f32[128,16,128]{2,1,0:T(8,128)}, f32[128,16,128]{2,1,0:T(8,128)S(1)}, u32[]{:S(2)}) copy-start(f32[128,16,128]{2,1,0:T(8,128)S(1)} %all-to-all-done) | copy-start | bytes 3145732

commit v3 on v2

--- a/solution.py
+++ b/solution.py
@@ -222,7 +222,7 @@
     return (base, base + (1 << rest))
 
 
-def levels(place, load, cos_of, sin_of, lhs_refs, w_ref, emit, before_level, beside):
+def levels(place, load, cos_of, sin_of, lhs_refs, w_ref, emit, before_stage, beside):
     signs = turn_signs()
 
     def build(step, quarter, lhs_ref):
@@ -264,8 +264,7 @@
 
     always = lax.axis_index("sx") >= 0
     for n in range(17):
-        if n % 4 == 0 and n < 16:
-            before_level(n // 4)
+        before_stage(n)
         pl.when(always)(functools.partial(stage, n))
 
 
@@ -341,7 +340,7 @@
         (lhs0, lhs1),
         w_ref,
         emit,
-        lambda step: None,
+        lambda n: None,
         beside,
     )
 
@@ -368,15 +367,16 @@
 
 def after_kernel(x_ref, w_hbm, turns_hbm, out_ref, w_ref, turns_ref, d0, d1, lhs0, lhs1, sems):
     steps = LEVELS - HALF
+    quarter = STEP_ROWS // 4
+    ends = [0, quarter] + [STEP_ROWS * (k + 1) for k in range(steps - 1)] + [PHASE_ROWS]
     copies = []
-    for k in range(steps):
-        first = k * STEP_ROWS
-        rows = pl.ds(first, STEP_ROWS if k < steps - 1 else PHASE_ROWS - first)
-        copies.append([pltpu.make_async_copy(turns_hbm.at[:, rows], turns_ref.at[:, rows], sems.at[k])])
-    copies[0].append(pltpu.make_async_copy(w_hbm, w_ref, sems.at[steps]))
-    for group in copies:
-        for copy in group:
-            copy.start()
+    for k in range(steps + 1):
+        rows = pl.ds(ends[k], ends[k + 1] - ends[k])
+        copies.append(pltpu.make_async_copy(turns_hbm.at[:, rows], turns_ref.at[:, rows], sems.at[k]))
+    copy_w = pltpu.make_async_copy(w_hbm, w_ref, sems.at[steps + 1])
+    copies[0].start()
+    copy_w.start()
+    copies[1].start()
     signs = turn_signs()
     refs = (x_ref, d0, d1, d0, out_ref)
 
@@ -397,9 +397,16 @@
             pos = place(i1, i2) * 8
             refs[step + 1][pos : pos + 8, :] = value
 
-    def before_level(step):
-        for copy in copies[step]:
-            copy.wait()
+    def before_stage(n):
+        if n == 0:
+            copies[0].wait()
+            for copy in copies[2:]:
+                copy.start()
+        if n == 1:
+            copy_w.wait()
+            copies[1].wait()
+        if n in (4, 8, 12):
+            copies[1 + n // 4].wait()
 
     levels(
         place,
@@ -409,29 +416,29 @@
         (lhs0, lhs1),
         w_ref,
         emit,
-        before_level,
+        before_stage,
         lambda step, quarter: None,
     )
 
 
 def order_kernel(x_ref, out_ref):
     lower = lax.broadcasted_iota(jnp.int32, (8, LANES), 1) < RANK
-    part = pl.program_id(0)
 
     @pl.loop(0, 8)
     def _(sx):
         for b4 in range(2):
-            for pair in range(2):
-                cols = slice(pair * LANES, (pair + 1) * LANES)
-                for h in range(2):
-                    start = ((sx * 16 + 8 * h) * 2 + b4) * 8 + part * 4 + 2 * pair
-                    a = x_ref[pl.ds(start, 8, stride=16), :]
-                    b = x_ref[pl.ds(start + 1, 8, stride=16), :]
-                    first = jnp.where(lower, a, pltpu.roll(b, RANK, 1))
-                    second = jnp.where(lower, pltpu.roll(a, RANK, 1), b)
-                    rows = slice(8 * h, 8 * h + 8)
-                    out_ref[0, pl.ds(b4 * 16 + sx, 1), rows, cols] = first[None]
-                    out_ref[0, pl.ds(b4 * 16 + 8 + sx, 1), rows, cols] = second[None]
+            for part in range(2):
+                for pair in range(2):
+                    cols = slice(pair * LANES, (pair + 1) * LANES)
+                    for h in range(2):
+                        start = ((sx * 16 + 8 * h) * 2 + b4) * 8 + part * 4 + 2 * pair
+                        a = x_ref[pl.ds(start, 8, stride=16), :]
+                        b = x_ref[pl.ds(start + 1, 8, stride=16), :]
+                        first = jnp.where(lower, a, pltpu.roll(b, RANK, 1))
+                        second = jnp.where(lower, pltpu.roll(a, RANK, 1), b)
+                        rows = slice(8 * h, 8 * h + 8)
+                        out_ref[part, pl.ds(b4 * 16 + sx, 1), rows, cols] = first[None]
+                        out_ref[part, pl.ds(b4 * 16 + 8 + sx, 1), rows, cols] = second[None]
 
 
 VMEM = pl.BlockSpec(memory_space=pltpu.VMEM)
@@ -495,9 +502,9 @@
             values,
             lhs,
             lhs,
-            pltpu.SemaphoreType.DMA((LEVELS - HALF + 1,)),
+            pltpu.SemaphoreType.DMA((LEVELS - HALF + 2,)),
         ],
-        compiler_params=pltpu.CompilerParams(vmem_limit_bytes=59 * MIB),
+        compiler_params=pltpu.CompilerParams(vmem_limit_bytes=57 * MIB),
         cost_estimate=cost(flops=4 * 2**31, bytes_accessed=8 * MIB),
         name="after",
     )(moved.reshape(ROWS, LANES), w, phases)
@@ -507,9 +514,8 @@
     return pl.pallas_call(
         order_kernel,
         out_shape=jax.ShapeDtypeStruct(weights.shape, F32),
-        grid=(2,),
         in_specs=[VMEM],
-        out_specs=pl.BlockSpec((1, *weights.shape[1:]), lambda part: (part, 0, 0, 0)),
+        out_specs=VMEM,
         compiler_params=pltpu.CompilerParams(vmem_limit_bytes=8 * MIB),
         cost_estimate=cost(flops=2**20, bytes_accessed=2 * MIB),
         name="order",

time: 77.8 us -> 77.3 us (level)
  no operation moved by 1% of the time
where the time goes in v3:
time: 77.3 us; the launch traced here: 77 us
  Pallas kernels  25.5 us (33%)
  blocking collectives  23.9 us (31%)
  waiting for transfers between devices  13 us (17%)
  starting transfers between devices  11.5 us (15%)
  local copies, waits for them, and re-layouts  2.99 us (4%)
    all_to_all x1, blocking collectives, local(): lax.all_to_all(after.reshape(128, 16, LANES), ('sx', 'sy'), 0, 0, tiled=T...  23.9 us
    all_to_all x1, waiting for transfers between devices, local(): lax.all_to_all(before.reshape(128, 16, LANES), ('sx', 'sy'), 0, 0, tiled=...  13 us
    all_to_all x1, starting transfers between devices, local(): lax.all_to_all(before.reshape(128, 16, LANES), ('sx', 'sy'), 0, 0, tiled=...  11.5 us
    pallas_call x1, Pallas kernels, local(): pl.pallas_call(before_kernel, out_shape=shape, in_specs=[HBM, HBM], out_s...  10.2 us
    pallas_call x1, Pallas kernels, local(): pl.pallas_call(after_kernel, out_shape=shape, in_specs=[VMEM, HBM, HBM],...  9.6 us
    pallas_call x1, Pallas kernels, local(): pl.pallas_call(phases_kernel, out_shape=phase, in_specs=[], out_specs=VME...  3.88 us
    unnamed x4, local copies, waits for them, and re-layouts  2.99 us
    pallas_call x1, Pallas kernels, local(): pl.pallas_call(order_kernel, out_shape=jax.ShapeDtypeStruct(weights.shape...  1.82 us
  transfers between devices with their start and end apart: 1, of which 1 were waited for; matrix products, arithmetic and copies ran while one was open for 0% of the time, Pallas kernels for 5%

profile of v3, /device:TPU:1, one launch (start us, length us, event | category | flops | bytes accessed | tf_op | source)
XLA Modules:
  0.0 77.0 jit_solution(17244161378760507914)
XLA Ops:
  0.0 10.2 %before.1 = f32[2048,128]{1,0:T(8,128)} custom-call(f32[2,32,16,256]{3,2,1,0:T(8,128)} %x_hbm.1, bf16[1024,256]{1,0:T(8,128)(2,1)} %constant.2.clone.w_hbm), custom_call_target="tpu_custom_call" | custom-call | flops 8589934592 | bytes 3145728 | tf_op jit(solution)/shard_map/before/pallas_call | solution.py:458
  10.2 11.5 %all-to-all-start = ((f32[128,16,128]{2,1,0:T(8,128)}), f32[128,16,128]{2,1,0:T(8,128)S(1)}, u32[]{:S(2)}, u32[]{:S(2)}) async-start(f32[128,16,128]{2,1,0:T(8,128)} %bitcast.6), calls=%async_computation | async-start | bytes 2097152 | tf_op jit(solution)/shard_map/all_to_all | solution.py:479
  21.7 3.9 %phases.1.turns_hbm = f32[2,4352,128]{2,1,0:T(8,128)S(1)} custom-call(), custom_call_target="tpu_custom_call" | custom-call | flops 8589934592 | bytes 5242880 | tf_op jit(solution)/shard_map/phases/pallas_call | solution.py:482
  25.6 0.0 copy-start
  25.6 2.0 %copy-done = f32[2,4352,128]{2,1,0:T(8,128)} copy-done((f32[2,4352,128]{2,1,0:T(8,128)}, f32[2,4352,128]{2,1,0:T(8,128)S(1)}, u32[]{:S(2)}) %copy-start) | copy-done | bytes 4456472
  27.6 13.0 %all-to-all-done = f32[128,16,128]{2,1,0:T(8,128)S(1)} async-done(((f32[128,16,128]{2,1,0:T(8,128)}), f32[128,16,128]{2,1,0:T(8,128)S(1)}, u32[]{:S(2)}, u32[]{:S(2)}) %all-to-all-start) | async-done | bytes 1048608 | tf_op jit(solution)/shard_map/all_to_all | solution.py:479
  40.6 0.0 copy-start.1
  40.6 1.0 %copy-done.1 = f32[128,16,128]{2,1,0:T(8,128)} copy-done((f32[128,16,128]{2,1,0:T(8,128)}, f32[128,16,128]{2,1,0:T(8,128)S(1)}, u32[]{:S(2)}) %copy-start.1) | copy-done | bytes 1048600
  41.6 9.6 %after.1 = f32[2048,128]{1,0:T(8,128)} custom-call(f32[2048,128]{1,0:T(8,128)} %bitcast.5, bf16[1024,256]{1,0:T(8,128)(2,1)} %constant.2.clone.w_hbm, f32[2,4352,128]{2,1,0:T(8,128)} %copy-done), custom_call_target="tpu_custom_call" | custom-call | flops 8589934592 | bytes 8388608 | tf_op jit(solution)/shard_map/after/pallas_call | solution.py:493
  51.2 23.9 %all_to_all.10 = f32[128,16,128]{2,1,0:T(8,128)S(1)} all-to-all(f32[128,16,128]{2,1,0:T(8,128)} %bitcast.7), channel_id=1, replica_groups=mesh['sx'=8,'sy'=16] {'sx','sy'}, dimensions={0} | all-to-all | bytes 2097152 | tf_op jit(solution)/shard_map/all_to_all | solution.py:512
  75.1 1.8 %order.1 = f32[2,32,16,256]{3,2,1,0:T(8,128)} custom-call(f32[2048,128]{1,0:T(8,128)S(1)} %bitcast.4), custom_call_target="tpu_custom_call" | custom-call | flops 1048576 | bytes 2097152 | tf_op jit(solution)/shard_map/order/pallas_call | solution.py:514
Async XLA Ops:
  10.2 30.4 %all-to-all-start = ((f32[128,16,128]{2,1,0:T(8,128)}), f32[128,16,128]{2,1,0:T(8,128)S(1)}, u32[]{:S(2)}, u32[]{:S(2)}) async-start(f32[128,16,128]{2,1,0:T(8,128)} %bitcast.6), calls=%async_computation | async-start | bytes 2097152 | tf_op jit(solution)/shard_map/all_to_all | solution.py:479
  25.6 2.0 %copy-start = (f32[2,4352,128]{2,1,0:T(8,128)}, f32[2,4352,128]{2,1,0:T(8,128)S(1)}, u32[]{:S(2)}) copy-start(f32[2,4352,128]{2,1,0:T(8,128)S(1)} %phases.1.turns_hbm) | copy-start | bytes 13369348
  40.6 1.0 %copy-start.1 = (f32[128,16,128]{2,1,0:T(8,128)}, f32[128,16,128]{2,1,0:T(8,128)S(1)}, u32[]{:S(2)}) copy-start(f32[128,16,128]{2,1,0:T(8,128)S(1)} %all-to-all-done) | copy-start | bytes 3145732

commit v4 on v3

--- a/solution.py
+++ b/solution.py
@@ -504,7 +504,7 @@
             lhs,
             pltpu.SemaphoreType.DMA((LEVELS - HALF + 2,)),
         ],
-        compiler_params=pltpu.CompilerParams(vmem_limit_bytes=57 * MIB),
+        compiler_params=pltpu.CompilerParams(vmem_limit_bytes=48 * MIB),
         cost_estimate=cost(flops=4 * 2**31, bytes_accessed=8 * MIB),
         name="after",
     )(moved.reshape(ROWS, LANES), w, phases)

time: 77.3 us -> 73 us (0.944)
  Pallas kernels: 25.5 us -> 23.2 us
  local copies, waits for them, and re-layouts: 2.99 us -> 2.03 us
  blocking collectives: 23.9 us -> 23.1 us
    pallas_call x1, Pallas kernels: 9.6 us -> 7.26 us  [local(): pl.pallas_call(after_kernel, out_shape=shape, in_specs=[VMEM, HBM, HBM],...]
    unnamed x4, local copies, waits for them, and re-layouts: 2.99 us -> 2.03 us
    all_to_all x1, blocking collectives: 23.9 us -> 23.1 us  [local(): lax.all_to_all(after.reshape(128, 16, LANES), ('sx', 'sy'), 0, 0, tiled=T...]
where the time goes in v4:
time: 73 us; the launch traced here: 72.8 us
  Pallas kernels  23.2 us (32%)
  blocking collectives  23.1 us (32%)
  waiting for transfers between devices  13 us (18%)
  starting transfers between devices  11.5 us (16%)
  local copies, waits for them, and re-layouts  2.03 us (3%)
    all_to_all x1, blocking collectives, local(): lax.all_to_all(after.reshape(128, 16, LANES), ('sx', 'sy'), 0, 0, tiled=T...  23.1 us
    all_to_all x1, waiting for transfers between devices, local(): lax.all_to_all(before.reshape(128, 16, LANES), ('sx', 'sy'), 0, 0, tiled=...  13 us
    all_to_all x1, starting transfers between devices, local(): lax.all_to_all(before.reshape(128, 16, LANES), ('sx', 'sy'), 0, 0, tiled=...  11.5 us
    pallas_call x1, Pallas kernels, local(): pl.pallas_call(before_kernel, out_shape=shape, in_specs=[HBM, HBM], out_s...  10.2 us
    pallas_call x1, Pallas kernels, local(): pl.pallas_call(after_kernel, out_shape=shape, in_specs=[VMEM, HBM, HBM],...  7.26 us
    pallas_call x1, Pallas kernels, local(): pl.pallas_call(phases_kernel, out_shape=phase, in_specs=[], out_specs=VME...  3.88 us
    unnamed x4, local copies, waits for them, and re-layouts  2.03 us
    pallas_call x1, Pallas kernels, local(): pl.pallas_call(order_kernel, out_shape=jax.ShapeDtypeStruct(weights.shape...  1.82 us
  transfers between devices with their start and end apart: 1, of which 1 were waited for; matrix products, arithmetic and copies ran while one was open for 0% of the time, Pallas kernels for 5%

profile of v4, /device:TPU:1, one launch (start us, length us, event | category | flops | bytes accessed | tf_op | source)
XLA Modules:
  0.0 72.8 jit_solution(1970819192114027872)
XLA Ops:
  0.0 10.2 %before.1 = f32[2048,128]{1,0:T(8,128)} custom-call(f32[2,32,16,256]{3,2,1,0:T(8,128)} %x_hbm.1, bf16[1024,256]{1,0:T(8,128)(2,1)} %constant.2.clone.w_hbm), custom_call_target="tpu_custom_call" | custom-call | flops 8589934592 | bytes 3145728 | tf_op jit(solution)/shard_map/before/pallas_call | solution.py:458
  10.2 11.5 %all-to-all-start = ((f32[128,16,128]{2,1,0:T(8,128)}), f32[128,16,128]{2,1,0:T(8,128)S(1)}, u32[]{:S(2)}, u32[]{:S(2)}) async-start(f32[128,16,128]{2,1,0:T(8,128)} %bitcast.7), calls=%async_computation | async-start | bytes 2097152 | tf_op jit(solution)/shard_map/all_to_all | solution.py:479
  21.7 0.0 copy-start
  21.7 3.9 %phases.1.turns_hbm = f32[2,4352,128]{2,1,0:T(8,128)S(1)} custom-call(), custom_call_target="tpu_custom_call" | custom-call | flops 8589934592 | bytes 5242880 | tf_op jit(solution)/shard_map/phases/pallas_call | solution.py:482
  25.6 0.0 copy-start.1
  25.6 2.0 %copy-done.1 = f32[2,4352,128]{2,1,0:T(8,128)} copy-done((f32[2,4352,128]{2,1,0:T(8,128)}, f32[2,4352,128]{2,1,0:T(8,128)S(1)}, u32[]{:S(2)}) %copy-start.1) | copy-done | bytes 4456472
  27.7 13.0 %all-to-all-done = f32[128,16,128]{2,1,0:T(8,128)S(1)} async-done(((f32[128,16,128]{2,1,0:T(8,128)}), f32[128,16,128]{2,1,0:T(8,128)S(1)}, u32[]{:S(2)}, u32[]{:S(2)}) %all-to-all-start) | async-done | bytes 1048608 | tf_op jit(solution)/shard_map/all_to_all | solution.py:479
  40.6 0.0 copy-done
  40.6 7.3 %after.1 = f32[2048,128]{1,0:T(8,128)S(1)} custom-call(f32[2048,128]{1,0:T(8,128)S(1)} %bitcast.5, bf16[1024,256]{1,0:T(8,128)(2,1)S(1)} %copy-done, f32[2,4352,128]{2,1,0:T(8,128)} %copy-done.1), custom_call_target="tpu_custom_call" | custom-call | flops 8589934592 | bytes 8388608 | tf_op jit(solution)/shard_map/after/pallas_call | solution.py:493
  47.9 23.1 %all_to_all.10 = f32[128,16,128]{2,1,0:T(8,128)S(1)} all-to-all(f32[128,16,128]{2,1,0:T(8,128)S(1)} %bitcast.6), channel_id=1, replica_groups=mesh['sx'=8,'sy'=16] {'sx','sy'}, dimensions={0} | all-to-all | bytes 2097152 | tf_op jit(solution)/shard_map/all_to_all | solution.py:512
  71.0 1.8 %order.1 = f32[2,32,16,256]{3,2,1,0:T(8,128)} custom-call(f32[2048,128]{1,0:T(8,128)S(1)} %bitcast.4), custom_call_target="tpu_custom_call" | custom-call | flops 1048576 | bytes 2097152 | tf_op jit(solution)/shard_map/order/pallas_call | solution.py:514
Async XLA Ops:
  10.2 30.4 %all-to-all-start = ((f32[128,16,128]{2,1,0:T(8,128)}), f32[128,16,128]{2,1,0:T(8,128)S(1)}, u32[]{:S(2)}, u32[]{:S(2)}) async-start(f32[128,16,128]{2,1,0:T(8,128)} %bitcast.7), calls=%async_computation | async-start | bytes 2097152 | tf_op jit(solution)/shard_map/all_to_all | solution.py:479
  21.7 18.9 %copy-start = (bf16[1024,256]{1,0:T(8,128)(2,1)S(1)}, bf16[1024,256]{1,0:T(8,128)(2,1)}, u32[]{:S(2)}) copy-start(bf16[1024,256]{1,0:T(8,128)(2,1)} %constant.2.clone.w_hbm) | copy-start | bytes 1572868
  25.6 2.0 %copy-start.1 = (f32[2,4352,128]{2,1,0:T(8,128)}, f32[2,4352,128]{2,1,0:T(8,128)S(1)}, u32[]{:S(2)}) copy-start(f32[2,4352,128]{2,1,0:T(8,128)S(1)} %phases.1.turns_hbm) | copy-start | bytes 13369348
